TPU v7x, 256 devices: a whole 4x4x8 slice. The times are simulated.
256 devices in a mesh: atoms: 32 (over x, y, core), kvec: 8 (over z).
Axes of the slice: x: 4, y: 4, z: 8, core: 2. Of those that a mesh axis runs over, the one named last changes fastest.
Arguments:
- positions: float32 [3, 131072], P(None, 'atoms'), may hold values from 0 to 1
- features: bfloat16 [131072, 128], P('atoms'), may hold values from -6 to 6
- charge_weight: bfloat16 [128, 32], replicated, may hold values from -0.5 to 0.5
- counts: int32 [32], P('atoms'), may hold values from 1 to 4096, 81920 in all
- mol_ids: int32 [32, 4096], P('atoms'), may hold values from 0 to 255, never falling along the last dimension, each value on 1 to 32 neighbouring positions
- energy_cot: float32 [8192], P('atoms'), may hold values from -6 to 6
- lattice: int32 [3, 8192], P(None, 'kvec'), may hold values from -12 to 12, as said below
- filter_in: bfloat16 [16, 256], replicated, may hold values from -1.5 to 1.5
- filter_mid: bfloat16 [256, 256], replicated, may hold values from -0.375 to 0.375
- filter_out: bfloat16 [256, 32], replicated, may hold values from -0.375 to 0.375
Outputs:
- mol_energy: float32 [8192], P('atoms')
- position_grad: float32 [3, 131072], P(None, ('atoms', 'kvec'))
- charge_grad: float32 [128, 32], replicated
- filter_in_grad: float32 [16, 256], replicated
- filter_mid_grad: float32 [256, 256], replicated
- filter_out_grad: float32 [256, 32], replicated
Inputs may be any that keep to these rules, and one draw needn't show every extreme that they name: `counts`: each group's count is at least 1 and at most 4096; some group holds exactly 4096 live atoms. `mol_ids`: within a group, ids never fall along the slots; each molecule has 1 to 32 slots; ids of dead slots are ignored. `lattice`: no k-vector has all three indices zero.
All inputs are finite; a program needn't handle non-finite values.
Results may differ from a plain program's by a relative error of at most 0.035.
Values may be sent and summed in bfloat16 or wider, within the bound.
A program may use at most 128 MiB of HBM per device.

v0:
```python
import math

import jax
import jax.numpy as jnp
from jax import lax
from jax.sharding import PartitionSpec as P

MAXN = 12


BOX_EDGE = 40.0


def contract_first(first_op, second_op):
    return lax.dot_general(
        first_op, second_op, (((0,), (0,)), ((), ())), preferred_element_type=jnp.float32
    )


def contract_last(first_op, second_op):
    return lax.dot_general(
        first_op, second_op, (((1,), (1,)), ((), ())), preferred_element_type=jnp.float32
    )


def slope(preact):
    sigmoid_val = jax.nn.sigmoid(preact)
    return sigmoid_val * (1.0 + preact * (1.0 - sigmoid_val))


def filter_pass(lattice, filter_in, filter_mid, filter_out, spectrum, total_atoms):
    channels = filter_out.shape[1]
    lattice_f = lattice.astype(jnp.float32)
    squared = jnp.sum(lattice_f * lattice_f, axis=0)
    inverse = 1.0 / (squared * math.sqrt(total_atoms))
    radius = jnp.sqrt(squared)
    num_basis = filter_in.shape[0]
    spacing = MAXN * math.sqrt(3.0) / num_basis
    centers = (jnp.arange(num_basis, dtype=jnp.float32) + 0.5) * spacing
    offset = (radius[None, :] - centers[:, None]) / spacing
    radial = jnp.exp(-0.5 * offset * offset).astype(jnp.bfloat16)
    pre_one = contract_first(filter_in, radial)
    act_one = jax.nn.silu(pre_one).astype(jnp.bfloat16)
    pre_two = contract_first(filter_mid, act_one)
    act_two = jax.nn.silu(pre_two).astype(jnp.bfloat16)
    logits = contract_first(filter_out, act_two)
    filters = (jax.nn.softplus(logits) * inverse[None, :]).T
    shaped = spectrum.reshape(spectrum.shape[0], 2, 2 * channels)
    spec_cos = shaped[:, 0, :channels]
    twin_cos = shaped[:, 0, channels:]
    spec_sin = shaped[:, 1, :channels]
    twin_sin = shaped[:, 1, channels:]
    coefficients = jnp.stack(
        [
            jnp.concatenate([filters * spec_cos, filters * twin_cos], axis=1),
            jnp.concatenate([filters * spec_sin, filters * twin_sin], axis=1),
        ],
        axis=1,
    ).astype(jnp.bfloat16)
    upstream = 0.5 * (spec_cos * twin_cos + spec_sin * twin_sin)
    grad_logits = (upstream.T * jax.nn.sigmoid(logits) * inverse[None, :]).astype(jnp.bfloat16)
    out_grad = contract_last(act_two, grad_logits)
    grad_two = (
        jnp.dot(filter_out, grad_logits, preferred_element_type=jnp.float32) * slope(pre_two)
    ).astype(jnp.bfloat16)
    mid_grad = contract_last(act_one, grad_two)
    grad_one = (
        jnp.dot(filter_mid, grad_two, preferred_element_type=jnp.float32) * slope(pre_one)
    ).astype(jnp.bfloat16)
    in_grad = contract_last(radial, grad_one)
    return (coefficients, in_grad, mid_grad, out_grad)


def body(
    positions,
    features,
    charge_weight,
    counts,
    mol_ids,
    energy_cot,
    lattice,
    filter_in,
    filter_mid,
    filter_out,
):
    capacity = features.shape[0]
    channels = charge_weight.shape[1]
    local_k = lattice.shape[1]
    molecules = energy_cot.shape[0]
    block_rows = max(min(512, capacity), capacity // 8)
    groups = lax.axis_size("atoms")
    total_atoms = capacity * groups
    slots = jnp.arange(capacity, dtype=jnp.int32)
    alive = (slots < counts[0]).astype(jnp.float32)
    member = (mol_ids[0][:, None] == jnp.arange(molecules, dtype=jnp.int32)[None, :]).astype(
        jnp.float32
    )
    weight_atom = jnp.dot(member, energy_cot, precision=lax.Precision.HIGHEST)
    charge = (
        jnp.dot(features, charge_weight, preferred_element_type=jnp.float32) * alive[:, None]
    ).astype(jnp.bfloat16)
    weighted = (weight_atom[:, None] * charge.astype(jnp.float32)).astype(jnp.bfloat16)
    paired = jnp.concatenate([charge, weighted], axis=1)
    wavevec = 2.0 * math.pi * lattice.astype(jnp.float32)
    live_count = counts[0]
    work_swap = jnp.concatenate([paired[:, channels:], paired[:, :channels]], axis=1)

    def phases(first_row):
        coords = positions[:, first_row : first_row + block_rows]
        angles = jnp.dot(coords.T, wavevec, precision=lax.Precision.HIGHEST)
        return jnp.stack([jnp.cos(angles), jnp.sin(angles)]).astype(jnp.bfloat16)

    def spectrum_term(phasors, first_row):
        return jnp.einsum(
            "sbk,bc->ksc",
            phasors,
            paired[first_row : first_row + block_rows],
            preferred_element_type=jnp.float32,
        )

    spectrum = jnp.zeros((local_k, 2, 2 * channels), jnp.float32)
    empty_term = jnp.zeros((local_k, 2, 2 * channels), jnp.float32)
    for block_index in range(capacity // block_rows):
        first_row = block_index * block_rows

        def only_term(first_row=first_row):
            return spectrum_term(phases(first_row), first_row)

        term = lax.cond(first_row < live_count, only_term, lambda: empty_term)
        spectrum = spectrum + term
    flattened = spectrum.reshape(local_k, 4 * channels)
    summed = lax.psum(flattened.astype(jnp.bfloat16), "atoms").astype(jnp.float32)
    coefficients, in_grad, mid_grad, out_grad = filter_pass(
        lattice, filter_in, filter_mid, filter_out, summed, total_atoms
    )

    def second_block(phasors, first_row):
        potentials = jnp.einsum(
            "sbk,ksc->bc", phasors, coefficients, preferred_element_type=jnp.float32
        )
        response = jnp.einsum(
            "bc,ksc->sbk",
            work_swap[first_row : first_row + block_rows],
            coefficients,
            preferred_element_type=jnp.float32,
        )
        angle_grad = 0.5 * (
            phasors[0].astype(jnp.float32) * response[1]
            - phasors[1].astype(jnp.float32) * response[0]
        )
        pos_grad = (
            lax.dot_general(
                wavevec,
                angle_grad,
                (((1,), (1,)), ((), ())),
                precision=lax.Precision.HIGHEST,
                preferred_element_type=jnp.float32,
            )
            / BOX_EDGE
        )
        return (potentials, pos_grad)

    empty_pair = (
        jnp.zeros((block_rows, 2 * channels), jnp.float32),
        jnp.zeros((3, block_rows), jnp.float32),
    )
    pot_parts = []
    grad_parts = []
    for block_index in range(capacity // block_rows):
        first_row = block_index * block_rows

        def second_fresh(first_row=first_row):
            return second_block(phases(first_row), first_row)

        potentials, pos_grad = lax.cond(first_row < live_count, second_fresh, lambda: empty_pair)
        pot_parts.append(potentials)
        grad_parts.append(pos_grad)
    pot_work = jnp.concatenate(pot_parts, axis=0)
    grad_work = jnp.concatenate(grad_parts, axis=1)
    potentials = pot_work
    volt = potentials[:, :channels]
    other = potentials[:, channels:]
    atom_energy = 0.5 * jnp.sum(charge.astype(jnp.float32) * volt, axis=1)
    mol_part = lax.dot_general(
        member,
        atom_energy,
        (((0,), (0,)), ((), ())),
        precision=lax.Precision.HIGHEST,
        preferred_element_type=jnp.float32,
    )
    charge_cot = (0.5 * (weight_atom[:, None] * volt + other) * alive[:, None]).astype(jnp.bfloat16)
    charge_part = contract_first(features, charge_cot)
    position_grad = lax.psum_scatter(
        grad_work.astype(jnp.bfloat16), "kvec", scatter_dimension=1, tiled=True
    ).astype(jnp.float32)
    charge_grad = lax.psum(charge_part, ("atoms", "kvec"))
    mol_energy, in_total, mid_total, out_total = (
        lax.psum(mol_part.astype(jnp.bfloat16), "kvec").astype(jnp.float32),
        lax.psum(in_grad.astype(jnp.bfloat16), "kvec").astype(jnp.float32),
        lax.psum(mid_grad.astype(jnp.bfloat16), "kvec").astype(jnp.float32),
        lax.psum(out_grad.astype(jnp.bfloat16), "kvec").astype(jnp.float32),
    )
    return (mol_energy, position_grad, charge_grad, in_total, mid_total, out_total)


def solution(mesh):
    return jax.shard_map(
        body,
        mesh=mesh,
        in_specs=(
            P(None, "atoms"),
            P("atoms", None),
            P(),
            P("atoms"),
            P("atoms", None),
            P("atoms"),
            P(None, "kvec"),
            P(),
            P(),
            P(),
        ),
        out_specs=(P("atoms"), P(None, ("atoms", "kvec")), P(), P(), P(), P()),
        check_vma=False,
    )
```

profile of v0, /device:TPU:2, one launch (start us, length us, event | category | flops | bytes accessed | tf_op | source)
XLA Modules:
  0.0 474.8 jit_solution(5942135080615568132)
XLA Ops:
  8.7 2.8 fusion.370
  12.9 11.1 %conditional.23 = (f32[1024,2,64]{0,2,1:T(8,128)S(1)}) conditional(s32[]{:T(128)} %convert_element_type.206, () %tuple.129, (f32[3,4096]{1,0:T(4,128)S(1)}, f32[3,1024]{1,0:T(4,128)S(1)}, bf16[4096,64]{0,1:T(8,128)(2,1)S(1)}) %tuple.224), branch_computations={%region_15.0_spmd, %region_16.0_spmd} | conditional | flops 158334976 | bytes 4808712 | solution.py:129
  12.9 10.6 %fusion.105 = (bf16[1,512,1024]{2,1,0:T(8,128)(2,1)S(1)}, bf16[1,512,1024]{2,1,0:T(8,128)(2,1)S(1)}) fusion(f32[3,1024]{1,0:T(4,128)S(1)} %get-tuple-element.158, f32[3,4096]{1,0:T(4,128)S(1)} %get-tuple-element.157), kind=kOutput, calls=%fused_computation.105 | convolution fusion | flops 19922944 | bytes 2121728 | tf_op jit(solution)/shard_map/cond/branch_1_fun/dot_general | solution.py:110
  24.0 11.1 %conditional.22 = (f32[1024,2,64]{0,2,1:T(8,128)S(1)}) conditional(s32[]{:T(128)} %convert_element_type.205, () %tuple.128, (f32[3,4096]{1,0:T(4,128)S(1)}, f32[3,1024]{1,0:T(4,128)S(1)}, bf16[4096,64]{0,1:T(8,128)(2,1)S(1)}) %tuple.225), branch_computations={%region_13.0_spmd, %region_14.0_spmd} | conditional | flops 158334976 | bytes 4808712 | solution.py:129
  24.0 10.6 %fusion.91 = (bf16[1,512,1024]{2,1,0:T(8,128)(2,1)S(1)}, bf16[1,512,1024]{2,1,0:T(8,128)(2,1)S(1)}) fusion(f32[3,1024]{1,0:T(4,128)S(1)} %get-tuple-element.155, f32[3,4096]{1,0:T(4,128)S(1)} %get-tuple-element.154), kind=kOutput, calls=%fused_computation.91 | convolution fusion | flops 19922944 | bytes 2121728 | tf_op jit(solution)/shard_map/cond/branch_1_fun/dot_general | solution.py:110
  35.1 11.9 %conditional.21 = (f32[1024,2,64]{0,2,1:T(8,128)S(1)}) conditional(s32[]{:T(128)} %convert_element_type.204, () %tuple.127, (f32[3,4096]{1,0:T(4,128)S(1)}, f32[3,1024]{1,0:T(4,128)S(1)}, bf16[4096,64]{0,1:T(8,128)(2,1)S(1)}) %tuple.226), branch_computations={%region_11.0_spmd, %region_12.0_spmd} | conditional | flops 158334976 | bytes 6905892 | solution.py:129
  35.1 10.6 %fusion.77 = (bf16[1,512,1024]{2,1,0:T(8,128)(2,1)S(1)}, bf16[1,512,1024]{2,1,0:T(8,128)(2,1)S(1)}) fusion(f32[3,1024]{1,0:T(4,128)S(1)} %get-tuple-element.152, f32[3,4096]{1,0:T(4,128)S(1)} %get-tuple-element.151), kind=kOutput, calls=%fused_computation.77 | convolution fusion | flops 19922944 | bytes 2121728 | tf_op jit(solution)/shard_map/cond/branch_1_fun/dot_general | solution.py:110
  47.0 12.7 %conditional.20 = (f32[1024,2,64]{0,2,1:T(8,128)}) conditional(s32[]{:T(128)} %convert_element_type.203, () %tuple.126, (f32[3,4096]{1,0:T(4,128)S(1)}, f32[3,1024]{1,0:T(4,128)S(1)}, bf16[4096,64]{0,1:T(8,128)(2,1)}) %tuple.227), branch_computations={%region_9.0_spmd, %region_10.0_spmd} | conditional | flops 158334976 | bytes 4808712 | solution.py:129
  47.0 10.6 %fusion.63 = (bf16[1,512,1024]{2,1,0:T(8,128)(2,1)S(1)}, bf16[1,512,1024]{2,1,0:T(8,128)(2,1)S(1)}) fusion(f32[3,1024]{1,0:T(4,128)S(1)} %get-tuple-element.149, f32[3,4096]{1,0:T(4,128)S(1)} %get-tuple-element.148), kind=kOutput, calls=%fused_computation.63 | convolution fusion | flops 19922944 | bytes 2121728 | tf_op jit(solution)/shard_map/cond/branch_1_fun/dot_general | solution.py:110
  59.8 12.7 %conditional.19 = (f32[1024,2,64]{0,2,1:T(8,128)}) conditional(s32[]{:T(128)} %convert_element_type.202, () %tuple.125, (f32[3,4096]{1,0:T(4,128)S(1)}, f32[3,1024]{1,0:T(4,128)S(1)}, bf16[4096,64]{0,1:T(8,128)(2,1)}) %tuple.228), branch_computations={%region_7.0_spmd, %region_8.0_spmd} | conditional | flops 158334976 | bytes 4808712 | solution.py:129
  59.8 10.5 %fusion.49 = (bf16[1,512,1024]{2,1,0:T(8,128)(2,1)S(1)}, bf16[1,512,1024]{2,1,0:T(8,128)(2,1)S(1)}) fusion(f32[3,1024]{1,0:T(4,128)S(1)} %get-tuple-element.146, f32[3,4096]{1,0:T(4,128)S(1)} %get-tuple-element.145), kind=kOutput, calls=%fused_computation.49 | convolution fusion | flops 19922944 | bytes 2121728 | tf_op jit(solution)/shard_map/cond/branch_1_fun/dot_general | solution.py:110
  72.4 12.7 %conditional.18 = (f32[1024,2,64]{0,2,1:T(8,128)}) conditional(s32[]{:T(128)} %convert_element_type.201, () %tuple.124, (f32[3,4096]{1,0:T(4,128)S(1)}, f32[3,1024]{1,0:T(4,128)S(1)}, bf16[4096,64]{0,1:T(8,128)(2,1)}) %tuple.229), branch_computations={%region_5.0_spmd, %region_6.0_spmd} | conditional | flops 158334976 | bytes 4808712 | solution.py:129
  72.4 10.6 %fusion.35 = (bf16[1,512,1024]{2,1,0:T(8,128)(2,1)S(1)}, bf16[1,512,1024]{2,1,0:T(8,128)(2,1)S(1)}) fusion(f32[3,1024]{1,0:T(4,128)S(1)} %get-tuple-element.139, f32[3,4096]{1,0:T(4,128)S(1)} %get-tuple-element.138), kind=kOutput, calls=%fused_computation.35 | convolution fusion | flops 19922944 | bytes 2121728 | tf_op jit(solution)/shard_map/cond/branch_1_fun/dot_general | solution.py:110
  85.1 13.1 %conditional.17 = (f32[1024,2,64]{0,2,1:T(8,128)}) conditional(s32[]{:T(128)} %convert_element_type.200, () %tuple.123, (f32[3,4096]{1,0:T(4,128)S(1)}, f32[3,1024]{1,0:T(4,128)S(1)}, bf16[4096,64]{0,1:T(8,128)(2,1)}) %tuple.230), branch_computations={%region_3.0_spmd, %region_4.0_spmd} | conditional | flops 158334976 | bytes 4808712 | solution.py:129
  85.6 10.6 %fusion.21 = (bf16[1,512,1024]{2,1,0:T(8,128)(2,1)S(1)}, bf16[1,512,1024]{2,1,0:T(8,128)(2,1)S(1)}) fusion(f32[3,1024]{1,0:T(4,128)S(1)} %get-tuple-element.136, f32[3,4096]{1,0:T(4,128)S(1)} %get-tuple-element.131), kind=kOutput, calls=%fused_computation.21 | convolution fusion | flops 19922944 | bytes 2121728 | tf_op jit(solution)/shard_map/cond/branch_1_fun/dot_general | solution.py:110
  98.3 12.7 %conditional.16 = (f32[1024,2,64]{0,2,1:T(8,128)}) conditional(s32[]{:T(128)} %convert_element_type.194, () %tuple.121, (f32[3,4096]{1,0:T(4,128)S(1)}, f32[3,1024]{1,0:T(4,128)S(1)}, bf16[4096,64]{0,1:T(8,128)(2,1)}) %tuple.231), branch_computations={%region_1.0_spmd, %region_2.0_spmd} | conditional | flops 158334976 | bytes 4808712 | solution.py:129
  98.3 10.6 %fusion.7 = (bf16[1,512,1024]{2,1,0:T(8,128)(2,1)S(1)}, bf16[1,512,1024]{2,1,0:T(8,128)(2,1)S(1)}) fusion(f32[3,1024]{1,0:T(4,128)S(1)} %get-tuple-element.129, f32[3,4096]{1,0:T(4,128)S(1)} %get-tuple-element.128), kind=kOutput, calls=%fused_computation.7 | convolution fusion | flops 19922944 | bytes 2121728 | tf_op jit(solution)/shard_map/cond/branch_1_fun/dot_general | solution.py:110
  111.0 2.7 add_convert_fusion
  114.3 2.4 multiply_convert_fusion
  116.7 110.9 %all-reduce.4.cloned.1.call-done = bf16[1024,2,64]{0,2,1:T(8,128)(2,1)} async-done(((bf16[1024,2,64]{0,2,1:T(8,128)(2,1)}), bf16[1024,2,64]{0,2,1:T(8,128)(2,1)}) %all-reduce.4.cloned.1.call-update) | async-done | bytes 262160 | tf_op jit(solution)/shard_map/psum | solution.py:132
  231.7 2.3 fusion.378
  233.9 2.3 convolution_convert_fusion
  236.3 14.4 %conditional.31 = (f32[512,64]{0,1:T(8,128)S(1)}, bf16[3,512]{1,0:T(4,128)(2,1)S(1)}) conditional(s32[]{:T(128)} %convert_element_type.206, () %tuple.137, (f32[3,4096]{1,0:T(4,128)S(1)}, f32[3,1024]{1,0:T(4,128)S(1)}, bf16[1024,2,64]{0,2,1:T(8,128)(2,1)S(1)}, bf16[4096,64]{0,1:T(8,128)(2,1)S(1)}) %tuple.232), branch_computations={%region_32.33_spmd, %region_33.34_spmd} | conditional | flops 311430144 | bytes 15440912 | solution.py:175
  236.3 10.6 %fusion.359 = (bf16[1,512,1024]{2,1,0:T(8,128)(2,1)S(1)}, bf16[1,512,1024]{2,1,0:T(8,128)(2,1)S(1)}) fusion(f32[3,1024]{1,0:T(4,128)S(1)} %get-tuple-element.189, f32[3,4096]{1,0:T(4,128)S(1)} %get-tuple-element.188), kind=kOutput, calls=%fused_computation.327 | convolution fusion | flops 19922944 | bytes 2121728 | tf_op jit(solution)/shard_map/cond/branch_1_fun/dot_general | solution.py:110
  248.4 2.2 fusion.356
  250.7 14.5 %conditional.30 = (f32[512,64]{0,1:T(8,128)S(1)}, bf16[3,512]{1,0:T(4,128)(2,1)S(1)}) conditional(s32[]{:T(128)} %convert_element_type.205, () %tuple.136, (f32[3,4096]{1,0:T(4,128)S(1)}, f32[3,1024]{1,0:T(4,128)S(1)}, bf16[1024,2,64]{0,2,1:T(8,128)(2,1)S(1)}, bf16[4096,64]{0,1:T(8,128)(2,1)S(1)}) %tuple.233), branch_computations={%region_30.31_spmd, %region_31.32_spmd} | conditional | flops 311430144 | bytes 15440912 | solution.py:175
  250.8 10.6 %fusion.327 = (bf16[1,512,1024]{2,1,0:T(8,128)(2,1)S(1)}, bf16[1,512,1024]{2,1,0:T(8,128)(2,1)S(1)}) fusion(f32[3,1024]{1,0:T(4,128)S(1)} %get-tuple-element.185, f32[3,4096]{1,0:T(4,128)S(1)} %get-tuple-element.184), kind=kOutput, calls=%fused_computation.299 | convolution fusion | flops 19922944 | bytes 2121728 | tf_op jit(solution)/shard_map/cond/branch_1_fun/dot_general | solution.py:110
  262.9 2.2 fusion.324
  265.2 14.3 %conditional.29 = (f32[512,64]{0,1:T(8,128)S(1)}, bf16[3,512]{1,0:T(4,128)(2,1)S(1)}) conditional(s32[]{:T(128)} %convert_element_type.204, () %tuple.135, (f32[3,4096]{1,0:T(4,128)S(1)}, f32[3,1024]{1,0:T(4,128)S(1)}, bf16[1024,2,64]{0,2,1:T(8,128)(2,1)S(1)}, bf16[4096,64]{0,1:T(8,128)(2,1)S(1)}) %tuple.234), branch_computations={%region_28.29_spmd, %region_29.30_spmd} | conditional | flops 311430144 | bytes 15440912 | solution.py:175
  265.2 10.6 %fusion.295 = (bf16[1,512,1024]{2,1,0:T(8,128)(2,1)S(1)}, bf16[1,512,1024]{2,1,0:T(8,128)(2,1)S(1)}) fusion(f32[3,1024]{1,0:T(4,128)S(1)} %get-tuple-element.181, f32[3,4096]{1,0:T(4,128)S(1)} %get-tuple-element.180), kind=kOutput, calls=%fused_computation.271 | convolution fusion | flops 19922944 | bytes 2121728 | tf_op jit(solution)/shard_map/cond/branch_1_fun/dot_general | solution.py:110
  277.3 2.2 fusion.292
  279.5 14.6 %conditional.28 = (f32[512,64]{0,1:T(8,128)S(1)}, bf16[3,512]{1,0:T(4,128)(2,1)S(1)}) conditional(s32[]{:T(128)} %convert_element_type.203, () %tuple.134, (f32[3,4096]{1,0:T(4,128)S(1)}, f32[3,1024]{1,0:T(4,128)S(1)}, bf16[1024,2,64]{0,2,1:T(8,128)(2,1)S(1)}, bf16[4096,64]{0,1:T(8,128)(2,1)S(1)}) %tuple.235), branch_computations={%region_26.27_spmd, %region_27.28_spmd} | conditional | flops 311430144 | bytes 15440912 | solution.py:175
  279.7 10.6 %fusion.263 = (bf16[1,512,1024]{2,1,0:T(8,128)(2,1)S(1)}, bf16[1,512,1024]{2,1,0:T(8,128)(2,1)S(1)}) fusion(f32[3,1024]{1,0:T(4,128)S(1)} %get-tuple-element.177, f32[3,4096]{1,0:T(4,128)S(1)} %get-tuple-element.176), kind=kOutput, calls=%fused_computation.243 | convolution fusion | flops 19922944 | bytes 2121728 | tf_op jit(solution)/shard_map/cond/branch_1_fun/dot_general | solution.py:110
  291.8 2.2 fusion.260
  294.1 14.3 %conditional.27 = (f32[512,64]{0,1:T(8,128)S(1)}, bf16[3,512]{1,0:T(4,128)(2,1)S(1)}) conditional(s32[]{:T(128)} %convert_element_type.202, () %tuple.133, (f32[3,4096]{1,0:T(4,128)S(1)}, f32[3,1024]{1,0:T(4,128)S(1)}, bf16[1024,2,64]{0,2,1:T(8,128)(2,1)S(1)}, bf16[4096,64]{0,1:T(8,128)(2,1)S(1)}) %tuple.236), branch_computations={%region_24.25_spmd, %region_25.26_spmd} | conditional | flops 311430144 | bytes 15440912 | solution.py:175
  294.1 10.6 %fusion.231 = (bf16[1,512,1024]{2,1,0:T(8,128)(2,1)S(1)}, bf16[1,512,1024]{2,1,0:T(8,128)(2,1)S(1)}) fusion(f32[3,1024]{1,0:T(4,128)S(1)} %get-tuple-element.173, f32[3,4096]{1,0:T(4,128)S(1)} %get-tuple-element.172), kind=kOutput, calls=%fused_computation.215 | convolution fusion | flops 19922944 | bytes 2121728 | tf_op jit(solution)/shard_map/cond/branch_1_fun/dot_general | solution.py:110
  306.2 2.2 fusion.228
  308.4 14.6 %conditional.26 = (f32[512,64]{0,1:T(8,128)S(1)}, bf16[3,512]{1,0:T(4,128)(2,1)S(1)}) conditional(s32[]{:T(128)} %convert_element_type.201, () %tuple.132, (f32[3,4096]{1,0:T(4,128)S(1)}, f32[3,1024]{1,0:T(4,128)S(1)}, bf16[1024,2,64]{0,2,1:T(8,128)(2,1)S(1)}, bf16[4096,64]{0,1:T(8,128)(2,1)S(1)}) %tuple.237), branch_computations={%region_22.23_spmd, %region_23.24_spmd} | conditional | flops 311430144 | bytes 15440912 | solution.py:175
  308.7 10.6 %fusion.199 = (bf16[1,512,1024]{2,1,0:T(8,128)(2,1)S(1)}, bf16[1,512,1024]{2,1,0:T(8,128)(2,1)S(1)}) fusion(f32[3,1024]{1,0:T(4,128)S(1)} %get-tuple-element.169, f32[3,4096]{1,0:T(4,128)S(1)} %get-tuple-element.168), kind=kOutput, calls=%fused_computation.187 | convolution fusion | flops 19922944 | bytes 2121728 | tf_op jit(solution)/shard_map/cond/branch_1_fun/dot_general | solution.py:110
  320.8 2.2 fusion.196
  323.0 14.3 %conditional.25 = (f32[512,64]{0,1:T(8,128)S(1)}, bf16[3,512]{1,0:T(4,128)(2,1)S(1)}) conditional(s32[]{:T(128)} %convert_element_type.200, () %tuple.131, (f32[3,4096]{1,0:T(4,128)S(1)}, f32[3,1024]{1,0:T(4,128)S(1)}, bf16[1024,2,64]{0,2,1:T(8,128)(2,1)S(1)}, bf16[4096,64]{0,1:T(8,128)(2,1)S(1)}) %tuple.238), branch_computations={%region_20.21_spmd, %region_21.22_spmd} | conditional | flops 311430144 | bytes 15440912 | solution.py:175
  323.0 10.6 %fusion.167 = (bf16[1,512,1024]{2,1,0:T(8,128)(2,1)S(1)}, bf16[1,512,1024]{2,1,0:T(8,128)(2,1)S(1)}) fusion(f32[3,1024]{1,0:T(4,128)S(1)} %get-tuple-element.165, f32[3,4096]{1,0:T(4,128)S(1)} %get-tuple-element.164), kind=kOutput, calls=%fused_computation.159 | convolution fusion | flops 19922944 | bytes 2121728 | tf_op jit(solution)/shard_map/cond/branch_1_fun/dot_general | solution.py:110
  335.1 2.2 fusion.164
  337.4 14.6 %conditional.24 = (f32[512,64]{0,1:T(8,128)S(1)}, bf16[3,512]{1,0:T(4,128)(2,1)S(1)}) conditional(s32[]{:T(128)} %convert_element_type.194, () %tuple.120, (f32[3,4096]{1,0:T(4,128)S(1)}, f32[3,1024]{1,0:T(4,128)S(1)}, bf16[1024,2,64]{0,2,1:T(8,128)(2,1)S(1)}, bf16[4096,64]{0,1:T(8,128)(2,1)S(1)}) %tuple.239), branch_computations={%region_18.19_spmd, %region_19.20_spmd} | conditional | flops 311430144 | bytes 15440912 | solution.py:175
  337.7 10.6 %fusion.135 = (bf16[1,512,1024]{2,1,0:T(8,128)(2,1)S(1)}, bf16[1,512,1024]{2,1,0:T(8,128)(2,1)S(1)}) fusion(f32[3,1024]{1,0:T(4,128)S(1)} %get-tuple-element.161, f32[3,4096]{1,0:T(4,128)S(1)} %get-tuple-element.160), kind=kOutput, calls=%fused_computation.131 | convolution fusion | flops 19922944 | bytes 2121728 | tf_op jit(solution)/shard_map/cond/branch_1_fun/dot_general | solution.py:110
  356.0 30.2 %all-reduce = (bf16[256]{0:T(256)(128)(2,1)S(1)}, bf16[16,256]{1,0:T(8,128)(2,1)S(1)}, bf16[256,32]{0,1:T(8,128)(2,1)S(1)}) all-reduce(bf16[256]{0:T(256)(128)(2,1)S(1)} %convert_element_type.209, bf16[16,256]{1,0:T(8,128)(2,1)S(1)} %copy-done.13, ...), channel_id=1, replica_groups=mesh['atoms'=32,'kvec'=8] {'kvec'}, use_global_device_ids=true, to_apply=%region_35.36 | all-reduce | flops 12544 | bytes 50176 | tf_op jit(solution)/shard_map/psum | solution.py:198
  388.0 72.3 %psum.44 = f32[128,32]{0,1:T(8,128)} all-reduce(f32[128,32]{0,1:T(8,128)S(1)} %convolution_bitcast_fusion.12), channel_id=1, replica_groups=mesh['atoms'=32,'kvec'=8] {'atoms','kvec'}, use_global_device_ids=true, to_apply=%region_37.38 | all-reduce | flops 4096 | bytes 32768 | tf_op jit(solution)/shard_map/psum | solution.py:196
  461.9 4.2 all-reduce.6.cloned.1.call-done
  (108 shorter events, 42.7 us)
Async XLA Ops:
  7.2 4.4 copy-start
  7.2 220.4 %all-reduce.4.cloned.1.call-start = ((), (), s32[]{:S(2)}) async-start(), calls=%async_computation.1 | async-start | bytes 524288 | tf_op jit(solution)/shard_map/psum | solution.py:132
  8.7 4.2 copy-start.5
  12.9 22.2 %copy-start.1 = (bf16[4096,64]{0,1:T(8,128)(2,1)}, bf16[4096,64]{0,1:T(8,128)(2,1)S(1)}, u32[]{:S(2)}) copy-start(bf16[4096,64]{0,1:T(8,128)(2,1)S(1)} %get-tuple-element.279) | copy-start | bytes 1572868
  35.1 10.6 %copy-start.2 = (bf16[4096,64]{0,1:T(8,128)(2,1)}, bf16[4096,64]{0,1:T(8,128)(2,1)S(1)}, u32[]{:S(2)}) copy-start(bf16[4096,64]{0,1:T(8,128)(2,1)S(1)} %get-tuple-element.153) | copy-start | bytes 1572868 | tf_op jit(solution)/shard_map/cond
  111.0 2.8 copy-start.12
  113.7 346.5 %reduce-scatter.4.cloned.1.call-start = ((), (), s32[]{:S(2)}) async-start(), calls=%async_computation.3 | async-start | bytes 1179648
  114.2 114.4 %copy-start.14 = (bf16[256,32]{0,1:T(8,128)(2,1)S(1)}, bf16[256,32]{0,1:T(8,128)(2,1)}, u32[]{:S(2)}) copy-start(bf16[256,32]{0,1:T(8,128)(2,1)} %param.51) | copy-start | bytes 49156
  116.7 115.0 %copy-start.3 = (bf16[256,1024]{0,1:T(8,128)(2,1)}, bf16[256,1024]{0,1:T(8,128)(2,1)S(1)}, u32[]{:S(2)}) copy-start(bf16[256,1024]{0,1:T(8,128)(2,1)S(1)} %get-tuple-element.284) | copy-start | bytes 1572868
  227.6 2.8 copy-start.16
  229.7 0.6 copy-start.6
  233.9 2.3 copy-start.8
  233.9 2.3 copy-start.9
  233.9 2.3 copy-start.10
  233.9 2.3 copy-start.11
  352.3 2.0 copy-start.15
  352.6 3.1 copy-start.4
  352.6 3.1 copy-start.7
  352.6 3.3 copy-start.13
  354.2 111.9 %all-reduce.6.cloned.1.call-start = ((), (), s32[]{:S(2)}) async-start(), calls=%async_computation.2 | async-start | bytes 262144 | tf_op jit(solution)/shard_map/psum | solution.py:200
Sparse Core Ops, SparseCore 0:
  113.8 113.6 all-reduce.3
  354.3 38.0 reduce-scatter.3
  395.4 70.6 all-reduce.5
where the time goes:
time: 484 us; the launch traced here: 475 us
  matrix products  228 us (47%)
  waiting for transfers between devices  115 us (24%)
  blocking collectives  103 us (21%)
  between operations  15.4 us (3%)
  other arithmetic  8.83 us (2%)
    dot_general x16, matrix products, phases(): angles = jnp.dot(coords.T, wavevec, precision=lax.Precision.HIGHEST)  169 us
    psum x1, waiting for transfers between devices, body(): lax.psum(flattened.astype(jnp.bfloat16), 'atoms').astype(jnp.float32)  111 us
    psum x1, blocking collectives, body(): charge_grad = lax.psum(charge_part, ('atoms', 'kvec'))  72.3 us
    psum x1, blocking collectives, body(): lax.psum(mol_part.astype(jnp.bfloat16), 'kvec').astype(jnp.float32)  30.2 us
    dot_general x8, matrix products, second_block(): lax.dot_general(wavevec, angle_grad, (((1,), (1,)), ((), ())), precision=...  17.9 us
    dot_general x8, matrix products, spectrum_term(): jnp.einsum('sbk,bc->ksc', phasors, paired[first_row:first_row + block_row...  12.9 us
  transfers between devices with their start and end apart: 3, of which 2 were waited for; matrix products, arithmetic and copies ran while one was open for 2% of the time, Pallas kernels for 0%

commit v1 on v0

v1 whole, which is shorter than its diff:
```python
import functools
import math

import jax
import jax.numpy as jnp
import numpy as np
from jax import lax
from jax.experimental import pallas as pl
from jax.experimental.pallas import tpu as pltpu
from jax.sharding import PartitionSpec as P

MAXN = 12
BOX_EDGE = 40.0
MESH = pl.DeviceIdType.MESH
F32 = jnp.float32
BF16 = jnp.bfloat16

PLANE = 32
RING = 8
CAP = 4096
CH = 32
HID = 256
MOLS = 256
YZ = 640
XC = 256
HALF = 320
TILE = 512
TILES = CAP // TILE
CHIPS = 16
PAIR_ROWS = 80
BIG = 48
SMALL = 32
TABLE = 512
FAR_FIRST = (4, 3, 5, 2, 6, 1, 7)
MIB = 1 << 20


def row_of(y_index, z_index):
    if y_index is None and z_index is None:
        return 624
    if y_index is None:
        return 576 + z_index
    if z_index is None:
        return 600 + y_index
    return 24 * y_index + z_index


def half_plane():
    vectors = [(0, n3) for n3 in range(13)]
    return vectors + [(n2, n3) for n2 in range(1, 13) for n3 in range(-12, 13)]


def sign_matrix():
    def cosine(n):
        return None if n == 0 else n - 1

    def sine(n):
        return 12 + n - 1

    matrix = np.zeros((2 * HALF, YZ), np.float32)
    for index, (n2, n3) in enumerate(half_plane()):
        size, sign = abs(n3), (1.0 if n3 >= 0 else -1.0)
        matrix[index, row_of(cosine(n2), cosine(size))] = 1.0
        if n2 and size:
            matrix[index, row_of(sine(n2), sine(size))] = -sign
        if n2:
            matrix[HALF + index, row_of(sine(n2), cosine(size))] = 1.0
        if size:
            matrix[HALF + index, row_of(cosine(n2), sine(size))] = sign
    return matrix


def nt(first, second):
    return lax.dot_general(first, second, (((1,), (1,)), ((), ())), preferred_element_type=F32)


def tn(first, second):
    return lax.dot_general(first, second, (((0,), (0,)), ((), ())), preferred_element_type=F32)


def nn(first, second):
    return jnp.dot(first, second, preferred_element_type=F32)


def cos_turns(turns):
    frac = turns - jnp.floor(turns + 0.5)
    x = (2.0 * math.pi) * (0.25 - jnp.abs(frac))
    s = x * x
    poly = jnp.full_like(s, -1.0 / 39916800.0)
    for coefficient in (1.0 / 362880.0, -1.0 / 5040.0, 1.0 / 120.0, -1.0 / 6.0, 1.0):
        poly = poly * s + coefficient
    return x * poly


def rows_of_parts(value):
    high = value.astype(BF16).astype(F32)
    rest = value - high
    middle = rest.astype(BF16).astype(F32)
    low = rest - middle
    row = lax.broadcasted_iota(jnp.int32, (16, value.shape[1]), 0)
    parts = jnp.where(row == 0, high, jnp.where(row == 1, middle, jnp.where(row == 2, low, 0.0)))
    return parts.astype(BF16)


def yz_turns(coord):
    row = lax.broadcasted_iota(jnp.int32, (24, 1), 0)
    harmonic = jnp.where(row < 12, row + 1, row - 11).astype(F32)
    shift = jnp.where(row < 12, 0.0, 0.25)
    return harmonic * coord - shift, harmonic


def x_turns(coord, rank):
    row = lax.broadcasted_iota(jnp.int32, (8, 1), 0)
    harmonic = (2 * rank + lax.rem(row, 2)).astype(F32)
    shift = jnp.where(row < 2, 0.0, 0.25)
    return harmonic * coord - shift, harmonic


def lane_roll(value, shift):
    return pltpu.roll(value, shift % value.shape[1], 1)


def slope(preact, sigmoid_val):
    return sigmoid_val * (1.0 + preact * (1.0 - sigmoid_val))


def point_squares(rank, axis):
    dims = (2 * HALF, 1) if axis == 0 else (1, 2 * HALF)
    index = lax.broadcasted_iota(jnp.int32, dims, axis)
    n1 = (2 * rank + jnp.where(index >= HALF, 1, 0)).astype(F32)
    index = jnp.where(index >= HALF, index - HALF, index)
    later = (index - 13).astype(F32)
    n2 = jnp.where(index < 13, 0.0, 1.0 + jnp.floor((later + 0.5) * (1.0 / 25.0)))
    n3 = jnp.where(index < 13, index.astype(F32), later - 25.0 * (n2 - 1.0) - 12.0)
    return n1 * n1 + n2 * n2 + n3 * n3


def loop(low, high, action):
    def run(i, carry):
        action(i)
        return carry

    lax.fori_loop(low, high, run, 0)


def first_pass(rank, count, v, half):
    cot_parts = rows_of_parts(v.cot[...])
    for tile in range(half * TILES // 2, (half + 1) * TILES // 2):
        at = pl.ds(tile * TILE, TILE)
        slot = tile * TILE + lax.broadcasted_iota(jnp.int32, (1, TILE), 1)
        alive = jnp.where(slot < count, 1.0, 0.0)
        v.alive[:, at] = alive
        molecule = lax.broadcasted_iota(jnp.int32, (MOLS, TILE), 0)
        member = jnp.where(molecule == v.ids[:, at], 1.0, 0.0).astype(BF16)
        v.member[:, at] = member
        weight = jnp.sum(nn(cot_parts, member), axis=0, keepdims=True)
        v.weight[:, at] = weight
        charge = (nt(v.cw[...], v.feat[at, :]) * alive).astype(BF16).astype(F32)
        pair = jnp.concatenate([charge, weight * charge], axis=0).astype(BF16)
        v.pair[:, at] = pair
        pair = pair.astype(F32)
        turns2, _ = yz_turns(v.pos[1:2, at])
        turns3, _ = yz_turns(v.pos[2:3, at])
        turns1, _ = x_turns(v.pos[0:1, at], rank)
        v.u2[:, at] = cos_turns(turns2)
        v.u3[:, at] = cos_turns(turns3)
        v.u1[:, at] = cos_turns(turns1)
        u3 = v.u3[:, at]
        for two in range(12):
            first = v.u2[2 * two : 2 * two + 1, at] * u3
            second = v.u2[2 * two + 1 : 2 * two + 2, at] * u3
            rows = jnp.concatenate([first, second], axis=0).astype(BF16)
            v.b[48 * two : 48 * two + 48, at] = rows
        v.b[576:624, at] = jnp.concatenate([u3, v.u2[:, at]], axis=0).astype(BF16)
        row = lax.broadcasted_iota(jnp.int32, (16, TILE), 0)
        v.b[624:640, at] = jnp.where(row == 0, 1.0, 0.0).astype(BF16)
        for j in range(4):
            v.a[64 * j : 64 * j + 64, at] = (v.u1[j : j + 1, at] * pair).astype(BF16)


def structure_sum(v, half):
    at = pl.ds(half * CAP // 2, CAP // 2)
    return nt(v.b[:, at], v.a[:, at])


def network(squared, v):
    inverse = jnp.where(squared > 0.0, 1.0, 0.0) / (
        jnp.maximum(squared, 1.0) * math.sqrt(CAP * PLANE)
    )
    spacing = MAXN * math.sqrt(3.0) / 16
    center = (lax.broadcasted_iota(jnp.int32, (1, 16), 1).astype(F32) + 0.5) * spacing
    away = (jnp.sqrt(squared) - center) / spacing
    radial = jnp.exp(-0.5 * away * away).astype(BF16)
    pre_one = nn(radial, v.fin[...])
    sig_one = jax.nn.sigmoid(pre_one)
    act_one = (pre_one * sig_one).astype(BF16)
    pre_two = nn(act_one, v.fmid[...])
    sig_two = jax.nn.sigmoid(pre_two)
    act_two = (pre_two * sig_two).astype(BF16)
    logits = nn(act_two, v.fout_wide[...])
    return inverse, radial, pre_one, sig_one, act_one, pre_two, sig_two, act_two, logits


def filter_forward(rank, v):
    lane = lax.broadcasted_iota(jnp.int32, (CH, 128), 1)
    channel = lax.broadcasted_iota(jnp.int32, (CH, 128), 0)
    spread = jnp.where(lax.rem(lane, CH) == channel, 1.0, 0.0).astype(BF16)
    v.fout_wide[...] = tn(v.fout[...], spread).astype(BF16)
    values = network(point_squares(rank, 0), v)
    inverse, logits = values[0], values[-1]
    soft = jnp.maximum(logits, 0.0) + jnp.log1p(jnp.exp(-jnp.abs(logits)))
    soft = soft * inverse
    half_lane = lax.broadcasted_iota(jnp.int32, (HALF, 128), 1)
    v.filters[...] = jnp.where(half_lane < 64, soft[:HALF], soft[HALF:])


def table_forward(rank, v):
    table = lax.broadcasted_iota(jnp.int32, (TABLE, 1), 0).astype(F32)
    inverse, radial, pre_one, sig_one, act_one, pre_two, sig_two, act_two, logits = network(table, v)
    v.radial[...] = radial
    v.act_one[...] = act_one
    v.act_two[...] = act_two
    v.slope_one[...] = slope(pre_one, sig_one)
    v.slope_two[...] = slope(pre_two, sig_two)
    v.sigmoid[...] = jax.nn.sigmoid(logits) * inverse
    v.same[...] = jnp.where(table == point_squares(rank, 1), 1.0, 0.0).astype(BF16)


def multiplicities(rank, v):
    def chunk(index, total):
        k = v.lattice[index]
        k1, k2, k3 = k[0:1, :], k[1:2, :], k[2:3, :]
        back = k1 < 0
        k1 = jnp.where(back, -k1, k1)
        k2 = jnp.where(back, -k2, k2)
        k3 = jnp.where(back, -k3, k3)
        flip = (k2 < 0) | ((k2 == 0) & (k3 < 0))
        k2 = jnp.where(flip, -k2, k2)
        k3 = jnp.where(flip, -k3, k3)
        code = jnp.where(k2 == 0, k3, k2 * 25 + k3)
        width = k.shape[1]
        hit = lax.broadcasted_iota(jnp.int32, (HALF, width), 0) == code
        hit = jnp.where(hit, 1.0, 0.0).astype(BF16)
        row = lax.broadcasted_iota(jnp.int32, (16, width), 0)
        own = (k1 - 2 * rank) == lax.rem(row, 2)
        sign = jnp.where((row >= 2) & flip, -1.0, 1.0)
        select = jnp.where(own & (row < 4), sign, 0.0).astype(BF16)
        return total + nt(hit, select)

    counted = lax.fori_loop(0, RING, chunk, jnp.zeros((HALF, 16), F32))
    lane = lax.broadcasted_iota(jnp.int32, (HALF, 128), 1)
    v.both[...] = jnp.where(lane < 64, counted[:, 0:1], counted[:, 1:2])
    v.difference[...] = jnp.where(lane < 64, counted[:, 2:3], counted[:, 3:4])


def coefficients(v):
    signs = v.signs[...]
    total = jnp.concatenate([v.total[:YZ, :], v.total[YZ:, :]], axis=1)
    v.sums[...] = nn(signs, total)
    ncc, ncs = v.sums[:HALF, :128], v.sums[HALF:, :128]
    nsc, nss = v.sums[:HALF, 128:], v.sums[HALF:, 128:]
    filters = v.filters[...]
    fp, fd = filters * v.both[...], filters * v.difference[...]
    gcc = (fp * ncc - fd * nss).astype(BF16)
    gss = (fp * nss - fd * ncc).astype(BF16)
    gsc = (fp * nsc + fd * ncs).astype(BF16)
    gcs = (fp * ncs + fd * nsc).astype(BF16)
    v.coef[:HALF, :128] = gcc
    v.coef[HALF:, :128] = gcs
    v.coef[:HALF, 128:] = gsc
    v.coef[HALF:, 128:] = gss
    v.gt[...] = tn(v.coef[...], signs).astype(BF16)


def swapped_coefficients(v):
    g = nn(v.signs_t[...], v.coef[...])
    lane = lax.broadcasted_iota(jnp.int32, (YZ, XC), 1)
    swapped = jnp.where(lax.rem(lane, 64) < 32, lane_roll(g, -32), lane_roll(g, 32))
    v.gs[...] = swapped.astype(BF16)


def upstream_table(v):
    ncc, ncs = v.sums[:HALF, :128], v.sums[HALF:, :128]
    nsc, nss = v.sums[:HALF, 128:], v.sums[HALF:, 128:]
    tcc, tcs = lane_roll(ncc, -32), lane_roll(ncs, -32)
    tsc, tss = lane_roll(nsc, -32), lane_roll(nss, -32)
    upstream = 0.5 * (
        v.both[...] * (ncc * tcc + nss * tss + nsc * tsc + ncs * tcs)
        + v.difference[...] * (nsc * tcs + ncs * tsc - ncc * tss - nss * tcc)
    )
    upstream = jnp.concatenate([upstream, lane_roll(upstream, -64)], axis=0)
    lane = lax.broadcasted_iota(jnp.int32, (2 * HALF, 128), 1)
    upstream = jnp.where(lane < CH, upstream, 0.0)
    total = nn(v.same[0:128, :], upstream.astype(BF16))
    for group in range(1, 4):
        rows = v.same[128 * group : 128 * group + 128, :]
        total = total + nn(rows, lane_roll(upstream, 32 * group).astype(BF16))
    return total.astype(BF16)


def filter_backward(v):
    upstream = v.up_total[...].astype(F32)
    upstream = jnp.concatenate(
        [upstream] + [lane_roll(upstream, -32 * group) for group in range(1, 4)], axis=0
    )
    lane = lax.broadcasted_iota(jnp.int32, (TABLE, 128), 1)
    grad_logits = jnp.where(lane < CH, upstream * v.sigmoid[...], 0.0).astype(BF16)
    out_grad = tn(grad_logits, v.act_two[...])
    grad_two = (nt(grad_logits, v.fout_wide[...]) * v.slope_two[...]).astype(BF16)
    v.mid_grad[...] = tn(v.act_one[...], grad_two)
    grad_one = (nt(grad_two, v.fmid[...]) * v.slope_one[...]).astype(BF16)
    v.in_grad[...] = tn(v.radial[...], grad_one)
    v.out_grad[...] = out_grad[:CH]


GRAD_SCALE = 0.5 * 2.0 * math.pi / BOX_EDGE


def potential_pass(rank, v):
    for tile in range(TILES):
        at = pl.ds(tile * TILE, TILE)
        turns1, h1 = x_turns(v.pos[0:1, at], rank)
        d1 = h1 * cos_turns(turns1 + 0.25)
        u1 = v.u1[:, at]
        pair = v.pair[:, at].astype(F32)
        charge, weighted = pair[:CH], pair[CH:]
        w = nn(v.gt[...], v.b[:, at])
        pot = sum(u1[j : j + 1, :] * w[64 * j : 64 * j + 64, :] for j in range(4))
        potx = sum(d1[j : j + 1, :] * w[64 * j : 64 * j + 64, :] for j in range(4))
        volt, other = pot[:CH], pot[CH:]
        grad_x = jnp.sum(weighted * potx[:CH] + charge * potx[CH:], axis=0, keepdims=True)
        v.message[tile, 0:1, :] = grad_x * GRAD_SCALE
        v.energy[:, at] = 0.5 * jnp.sum(charge * volt, axis=0, keepdims=True)
        v.cot_rows[:, at] = (0.5 * (v.weight[:, at] * volt + other) * v.alive[:, at]).astype(BF16)
    return nn(v.cot_rows[...], v.feat[...])


def molecule_sums(v):
    return jnp.sum(nt(rows_of_parts(v.energy[...]), v.member[...]), axis=0, keepdims=True)


def force_pass(v):
    def fold(value):
        return value[0:8] + value[8:16] + value[16:24]

    for tile in range(TILES):
        at = pl.ds(tile * TILE, TILE)
        turns2, h2 = yz_turns(v.pos[1:2, at])
        turns3, h3 = yz_turns(v.pos[2:3, at])
        v.d2[:, at] = h2 * cos_turns(turns2 + 0.25)
        v.response[:, at] = nn(v.gs[...], v.a[:, at])
        u3, d3 = v.u3[:, at], h3 * cos_turns(turns3 + 0.25)
        sum_y = fold(v.d2[:, at] * v.response[600:624, at])
        sum_z = fold(d3 * v.response[576:600, at])
        for y in range(24):
            response = v.response[24 * y : 24 * y + 24, at]
            sum_y = sum_y + v.d2[y : y + 1, at] * fold(u3 * response)
            sum_z = sum_z + v.u2[y : y + 1, at] * fold(d3 * response)
        v.message[tile, 1:2, :] = jnp.sum(sum_y, axis=0, keepdims=True) * GRAD_SCALE
        v.message[tile, 2:3, :] = jnp.sum(sum_z, axis=0, keepdims=True) * GRAD_SCALE


SCRATCH = dict(
    pos=((3, CAP), F32), feat=((CAP, 128), BF16), cw=((CH, 128), BF16), ids=((1, CAP), jnp.int32),
    cot=((1, MOLS), F32), fin=((16, HID), BF16), fmid=((HID, HID), BF16), fout=((CH, HID), BF16),
    signs=((2 * HALF, YZ), BF16), signs_t=((YZ, 2 * HALF), BF16), lattice=((RING, 3, 1024), jnp.int32),
    u1=((8, CAP), F32), u2=((24, CAP), F32), u3=((24, CAP), F32), d2=((24, CAP), F32),
    alive=((1, CAP), F32), weight=((1, CAP), F32), member=((MOLS, CAP), BF16),
    pair=((2 * CH, CAP), BF16), b=((YZ, CAP), BF16), a=((XC, CAP), BF16), acc=((YZ, XC), F32),
    part=((2 * YZ, 128), BF16), mate=((YZ, 128), BF16), half=((YZ, 128), BF16),
    inbox=((CHIPS, BIG, 128), BF16), total=((2 * YZ, 128), BF16),
    radial=((TABLE, 16), BF16), act_one=((TABLE, HID), BF16), act_two=((TABLE, HID), BF16),
    slope_one=((TABLE, HID), F32), slope_two=((TABLE, HID), F32), fout_wide=((HID, 128), BF16),
    sigmoid=((TABLE, 128), F32), same=((TABLE, 2 * HALF), BF16), filters=((HALF, 128), F32),
    both=((HALF, 128), F32), difference=((HALF, 128), F32),
    sums=((2 * HALF, XC), F32), coef=((2 * HALF, XC), BF16), energy=((1, CAP), F32), cot_rows=((CH, CAP), BF16),
    gt=((XC, YZ), BF16), gs=((YZ, XC), BF16), response=((YZ, CAP), F32),
    up=((128, 128), BF16), up_ring=((RING, 64, 128), BF16), up_total=((128, 128), BF16),
    message=((RING, 4, TILE), F32), message_box=((RING, 4, TILE), F32),
    charge_ring=((RING, CH, 128), BF16), charge_mine=((CH, 128), BF16), charge_mate=((CH, 128), BF16),
    charge_plane=((CHIPS, CH, 128), BF16),
    mol_sum=((1, MOLS), F32), pos_sum=((3, TILE), F32), charge_sum=((CH, 128), F32),
    in_grad=((16, HID), F32), mid_grad=((HID, HID), F32), out_grad=((CH, HID), F32),
)
SEMAPHORES = dict(
    load=11, store=6, mate_s=4, mate_r=4, scatter_s=1, scatter_r=1, gather_s=1, gather_r=1,
    ring_s=4, ring_r=4, plane_s=1, plane_r=1,
)
OUTS = (
    ((1, MOLS), F32), ((3, TILE), F32), ((CH, 128), F32), ((16, HID), F32), ((HID, HID), F32), ((CH, HID), F32),
)


class Names:
    def __init__(self, names, refs):
        for name, ref in zip(names, refs, strict=True):
            setattr(self, name, ref)


def whole_kernel(
    count_ref, pos_ref, feat_ref, cw_ref, ids_ref, cot_ref, lattice_ref, fin_ref, fmid_ref, fout_ref,
    signs_ref, signs_t_ref, mol_out, pos_out, charge_out, in_out, mid_out, out_out, *scratch,
):
    v = Names(SCRATCH, scratch[: len(SCRATCH)])
    sem = Names(SEMAPHORES, scratch[len(SCRATCH) :])
    plane, ring = lax.axis_index("atoms"), lax.axis_index("kvec")
    chip, core = plane // 2, lax.rem(plane, 2)
    rank = ring

    loads = [
        pltpu.make_async_copy(src, dst, sem.load.at[i])
        for i, (src, dst) in enumerate((
            (pos_ref, v.pos), (feat_ref, v.feat), (cw_ref, v.cw), (ids_ref, v.ids), (cot_ref, v.cot),
            (lattice_ref, v.lattice.at[ring]), (fin_ref, v.fin), (fmid_ref, v.fmid), (fout_ref, v.fout),
            (signs_ref, v.signs), (signs_t_ref, v.signs_t),
        ))
    ]
    for load in loads:
        load.start()
    stores = [
        pltpu.make_async_copy(src, dst, sem.store.at[i])
        for i, (src, dst) in enumerate((
            (v.mol_sum, mol_out), (v.pos_sum, pos_out), (v.charge_sum, charge_out),
            (v.in_grad, in_out), (v.mid_grad, mid_out), (v.out_grad, out_out),
        ))
    ]

    def remote(src, dst, send, recv, device):
        return pltpu.make_async_remote_copy(
            src_ref=src, dst_ref=dst, send_sem=send, recv_sem=recv,
            device_id=device, device_id_type=MESH,
        )

    def await_bytes(ref, semaphore):
        pltpu.make_async_copy(ref, ref, semaphore).wait()

    def ring_peer(i):
        return (plane, lax.rem(ring + i, RING))

    def chip_device(which):
        return (2 * which + core, ring)

    mate = (plane + 1 - 2 * core, ring)

    barrier = pltpu.get_barrier_semaphore()

    def greet(device):
        pl.semaphore_signal(barrier, inc=1, device_id=device, device_id_type=MESH)

    loop(1, CHIPS, lambda i: greet(chip_device(lax.rem(chip + i, CHIPS))))
    loop(1, RING, lambda i: greet(ring_peer(i)))
    greet(mate)

    for load in loads[:5]:
        load.wait()
    first_pass(rank, count_ref[0], v, 0)
    for load in loads[5:]:
        load.wait()
    pl.semaphore_wait(barrier, CHIPS + RING - 1)

    def share(slots, phase):
        for i in FAR_FIRST:
            remote(slots.at[ring], slots.at[ring], sem.ring_s.at[phase], sem.ring_r.at[phase], ring_peer(i)).start()

    def shared(slots, phase):
        await_bytes(slots.at[pl.ds(0, RING - 1)], sem.ring_r.at[phase])

    share(v.lattice, 0)
    v.acc[...] = structure_sum(v, 0)
    first_pass(rank, count_ref[0], v, 1)
    structure = v.acc[...] + structure_sum(v, 1)
    v.part[:YZ, :] = structure[:, :128].astype(BF16)
    v.part[YZ:, :] = structure[:, 128:].astype(BF16)

    def half_rows(which):
        return pl.ds(pl.multiple_of(YZ * which, YZ), YZ)

    def to_mate(src, dst, phase):
        return remote(src, dst, sem.mate_s.at[phase], sem.mate_r.at[phase], mate)

    swap_parts = to_mate(v.part.at[half_rows(1 - core)], v.mate, 0)
    swap_parts.start()
    swap_parts.wait_recv()
    v.half[...] = (v.part[half_rows(core)].astype(F32) + v.mate[...].astype(F32)).astype(BF16)

    def pair_rows(which, odd, base=0):
        start = base + PAIR_ROWS * which + (BIG if odd else 0)
        return pl.ds(pl.multiple_of(start, 16), SMALL if odd else BIG)

    def scatter(pair, odd):
        size = SMALL if odd else BIG
        remote(
            v.half.at[pair_rows(pair, odd)], v.inbox.at[chip, pl.ds(0, size)],
            sem.scatter_s.at[0], sem.scatter_r.at[0], chip_device(2 * pair + odd),
        ).start()

    my_pair, my_odd = chip // 2, lax.rem(chip, 2)

    def scatter_pair(i):
        pair = lax.rem(my_pair + 1 + lax.rem(i + 3, 7), 8)
        scatter(pair, 0)
        scatter(pair, 1)

    loop(0, 7, scatter_pair)
    pl.when(my_odd == 0)(lambda: scatter(my_pair, 1))
    pl.when(my_odd == 1)(lambda: scatter(my_pair, 0))
    filter_forward(rank, v)
    table_forward(rank, v)

    def reduce(odd):
        size = SMALL if odd else BIG
        v.inbox[chip, :size] = v.half[pair_rows(my_pair, odd)]
        await_bytes(v.inbox.at[pl.ds(0, CHIPS - 1), pl.ds(0, size)], sem.scatter_r.at[0])
        value = v.inbox[0, :size].astype(F32)
        for slot in range(1, CHIPS):
            value = value + v.inbox[slot, :size].astype(F32)
        rows = pair_rows(my_pair, odd, YZ * core)
        v.total[rows] = value.astype(BF16)

        def send(i):
            other = lax.rem(chip + 1 + lax.rem(i + 5, 15), CHIPS)
            remote(
                v.total.at[rows], v.total.at[rows], sem.gather_s.at[0], sem.gather_r.at[0],
                chip_device(other),
            ).start()

        loop(0, CHIPS - 1, send)

    pl.when(my_odd == 0)(lambda: reduce(0))
    pl.when(my_odd == 1)(lambda: reduce(1))

    shared(v.lattice, 0)
    multiplicities(rank, v)

    def reduced(odd):
        size = SMALL if odd else BIG
        await_bytes(v.total.at[pl.ds(0, YZ - size)], sem.gather_r.at[0])
        await_bytes(v.total.at[pl.ds(0, YZ - size)], sem.scatter_s.at[0])

    pl.when(my_odd == 0)(lambda: reduced(0))
    pl.when(my_odd == 1)(lambda: reduced(1))
    swap_totals = to_mate(v.total.at[half_rows(core)], v.total.at[half_rows(core)], 1)
    swap_totals.start()
    swap_totals.wait_recv()

    coefficients(v)
    v.up[...] = upstream_table(v)
    v.up_ring[ring] = v.up[pl.ds(pl.multiple_of(64 * core, 64), 64), :]
    share(v.up_ring, 1)
    v.charge_ring[ring] = potential_pass(rank, v).astype(BF16)
    share(v.charge_ring, 2)
    molecules = molecule_sums(v)
    for chunk in range(RING):
        v.message[chunk, 3:4, 0:MOLS] = molecules
        v.message[chunk, 3:4, MOLS:TILE] = jnp.zeros((1, TILE - MOLS), F32)

    swapped_coefficients(v)
    force_pass(v)
    for i in FAR_FIRST:
        peer = lax.rem(ring + i, RING)
        remote(v.message.at[peer], v.message_box.at[ring], sem.ring_s.at[3], sem.ring_r.at[3], ring_peer(i)).start()
    v.message_box[ring] = v.message[ring]

    def added(slots):
        value = slots[0].astype(F32)
        for slot in range(1, slots.shape[0]):
            value = value + slots[slot].astype(F32)
        return value

    shared(v.up_ring, 1)
    up_rows = pl.ds(pl.multiple_of(64 * core, 64), 64)
    v.up_total[up_rows, :] = added(v.up_ring).astype(BF16)
    swap_up = to_mate(v.up_total.at[up_rows], v.up_total.at[up_rows], 2)
    swap_up.start()

    shared(v.charge_ring, 2)
    v.charge_mine[...] = added(v.charge_ring).astype(BF16)
    swap_charge = to_mate(v.charge_mine, v.charge_mate, 3)
    swap_charge.start()
    swap_charge.wait_recv()
    v.charge_plane[chip] = (v.charge_mine[...].astype(F32) + v.charge_mate[...].astype(F32)).astype(BF16)

    def charge_to_plane(i):
        other = lax.rem(chip + 1 + lax.rem(i + 5, 15), CHIPS)
        remote(
            v.charge_plane.at[chip], v.charge_plane.at[chip], sem.plane_s.at[0], sem.plane_r.at[0],
            chip_device(other),
        ).start()

    loop(0, CHIPS - 1, charge_to_plane)

    swap_up.wait_recv()
    filter_backward(v)
    for store in stores[3:]:
        store.start()
    shared(v.message_box, 3)
    value = added(v.message_box)
    v.pos_sum[...] = value[0:3]
    v.mol_sum[...] = value[3:4, :MOLS]
    for store in stores[:2]:
        store.start()

    for swap in (swap_parts, swap_totals, swap_up, swap_charge):
        swap.wait_send()
    for phase, slots in enumerate((v.lattice, v.up_ring, v.charge_ring, v.message)):
        await_bytes(slots.at[pl.ds(0, RING - 1)], sem.ring_s.at[phase])

    def gathered(odd):
        size = SMALL if odd else BIG
        await_bytes(v.inbox.at[pl.ds(0, CHIPS - 1), pl.ds(0, size)], sem.gather_s.at[0])

    pl.when(my_odd == 0)(lambda: gathered(0))
    pl.when(my_odd == 1)(lambda: gathered(1))
    await_bytes(v.charge_plane.at[pl.ds(0, CHIPS - 1)], sem.plane_s.at[0])

    await_bytes(v.charge_plane.at[pl.ds(0, CHIPS - 1)], sem.plane_r.at[0])
    v.charge_sum[...] = added(v.charge_plane)
    stores[2].start()
    for store in stores:
        store.wait()


def output_kernel(*refs):
    count = len(OUTS)
    sem = refs[-1]
    copies = [pltpu.make_async_copy(refs[i], refs[count + i], sem.at[i]) for i in range(count)]
    for copy in copies:
        copy.start()
    for copy in copies:
        copy.wait()


def specs(space, count):
    return [pl.BlockSpec(memory_space=space)] * count


def body(
    positions, features, charge_weight, counts, mol_ids, energy_cot,
    lattice, filter_in, filter_mid, filter_out,
):
    shape = jax.ShapeDtypeStruct
    dma = pltpu.SemaphoreType.DMA
    signs = jnp.asarray(sign_matrix(), BF16)
    signs_t = jnp.asarray(sign_matrix().T, BF16)
    outs = tuple(shape(*out) for out in OUTS)
    sums = pl.pallas_call(
        whole_kernel,
        out_shape=outs,
        in_specs=specs(pltpu.SMEM, 1) + specs(pl.ANY, 11),
        out_specs=tuple(specs(pl.ANY, len(OUTS))),
        scratch_shapes=[pltpu.VMEM(dims, kind) for dims, kind in SCRATCH.values()]
        + [dma((count,)) for count in SEMAPHORES.values()],
        compiler_params=pltpu.CompilerParams(
            collective_id=0, has_side_effects=True, vmem_limit_bytes=56 * MIB
        ),
        name="ewald",
    )(
        counts, positions, features, charge_weight.T, mol_ids, energy_cot.reshape(1, MOLS), lattice,
        filter_in, filter_mid, filter_out.T, signs, signs_t,
    )
    mol, pos, charge, first, middle, last = pl.pallas_call(
        output_kernel,
        out_shape=outs,
        in_specs=specs(pl.ANY, len(OUTS)),
        out_specs=tuple(specs(pl.ANY, len(OUTS))),
        scratch_shapes=[dma((len(OUTS),))],
        compiler_params=pltpu.CompilerParams(vmem_limit_bytes=56 * MIB),
        name="outputs",
    )(*sums)
    return (mol.reshape(MOLS), pos, charge.T, first, middle, last.T)


def solution(mesh):
    return jax.shard_map(
        body,
        mesh=mesh,
        in_specs=(
            P(None, "atoms"), P("atoms", None), P(), P("atoms"), P("atoms", None), P("atoms"),
            P(None, "kvec"), P(), P(), P(),
        ),
        out_specs=(P("atoms"), P(None, ("atoms", "kvec")), P(), P(), P(), P()),
        check_vma=False,
    )
```

time: 484 us -> 54.4 us (0.11)
  the two profiles are of different devices: /device:TPU:2 before, /device:TPU:1 now
where the time goes in v1:
time: 54.4 us; the launch traced here: 54.3 us
  Pallas kernels  52.8 us (97%)
  between operations  1.45 us (3%)
    pallas_call x1, Pallas kernels, body(): pl.pallas_call(whole_kernel, out_shape=outs, in_specs=specs(pltpu.SMEM, 1...  41.4 us
    pallas_call x1, Pallas kernels, body(): pl.pallas_call(output_kernel, out_shape=outs, in_specs=specs(pl.ANY, len(...  11.4 us

profile of v1, /device:TPU:1, one launch (start us, length us, event | category | flops | bytes accessed | tf_op | source)
XLA Modules:
  0.0 54.3 jit_solution(4539952621761395687)
XLA Ops:
  1.3 41.4 %ewald.1 = (f32[1,256]{1,0:T(1,128)}, f32[3,512]{1,0:T(4,128)}, f32[32,128]{1,0:T(8,128)}, f32[16,256]{1,0:T(8,128)}, f32[256,256]{1,0:T(8,128)}, /*index=5*/f32[32,256]{1,0:T(8,128)}) custom-call(s32[1]{0:T(128)S(6)} %copy.18.count_ref, f32[3,4096]{1,0:T(4,128)} %pos_ref.1, bf16[4096,128]{1,0:T(8,128)(2,1)} %feat_ref.1, bf16[32,128]{1,0:T(8,128)(2,1)} %bitcast.7, ...), custom_call_target="tpu_custom_call" | custom-call | tf_op jit(solution)/shard_map/ewald/pallas_call | solution.py:646
  42.7 11.4 %outputs.1 = (f32[1,256]{1,0:T(1,128)}, f32[3,512]{1,0:T(4,128)}, f32[32,128]{1,0:T(8,128)}, f32[16,256]{1,0:T(8,128)}, f32[256,256]{1,0:T(8,128)}, /*index=5*/f32[32,256]{1,0:T(8,128)}) custom-call(f32[1,256]{1,0:T(1,128)} %get-tuple-element.18.refs_0_, f32[3,512]{1,0:T(4,128)} %get-tuple-element.19.refs_1_, f32[32,128]{1,0:T(8,128)} %get-tuple-element.20.refs_2_, ...), custom_call_target="tpu_custom_call" | custom-call | tf_op jit(solution)/shard_map/outputs/pallas_call | solution.py:661

commit v2 on v1

--- a/solution.py
+++ b/solution.py
@@ -178,9 +178,9 @@
             v.a[64 * j : 64 * j + 64, at] = (v.u1[j : j + 1, at] * pair).astype(BF16)
 
 
-def structure_sum(v, half):
+def structure_sum(v, rows, half):
     at = pl.ds(half * CAP // 2, CAP // 2)
-    return nt(v.b[:, at], v.a[:, at])
+    return nt(v.b[rows, at], v.a[:, at])
 
 
 def network(squared, v):
@@ -255,7 +255,13 @@
 
 def coefficients(v):
     signs = v.signs[...]
-    total = jnp.concatenate([v.total[:YZ, :], v.total[YZ:, :]], axis=1)
+    total = jnp.concatenate(
+        [
+            jnp.concatenate([v.total[start : start + HALF], v.total[start + HALF : start + YZ]], axis=1)
+            for start in (0, YZ)
+        ],
+        axis=0,
+    )
     v.sums[...] = nn(signs, total)
     ncc, ncs = v.sums[:HALF, :128], v.sums[HALF:, :128]
     nsc, nss = v.sums[:HALF, 128:], v.sums[HALF:, 128:]
@@ -367,7 +373,7 @@
     u1=((8, CAP), F32), u2=((24, CAP), F32), u3=((24, CAP), F32), d2=((24, CAP), F32),
     alive=((1, CAP), F32), weight=((1, CAP), F32), member=((MOLS, CAP), BF16),
     pair=((2 * CH, CAP), BF16), b=((YZ, CAP), BF16), a=((XC, CAP), BF16), acc=((YZ, XC), F32),
-    part=((2 * YZ, 128), BF16), mate=((YZ, 128), BF16), half=((YZ, 128), BF16),
+    part=((YZ, 128), BF16), mate=((YZ, 128), BF16), half=((YZ, 128), BF16),
     inbox=((CHIPS, BIG, 128), BF16), total=((2 * YZ, 128), BF16),
     radial=((TABLE, 16), BF16), act_one=((TABLE, HID), BF16), act_two=((TABLE, HID), BF16),
     slope_one=((TABLE, HID), F32), slope_two=((TABLE, HID), F32), fout_wide=((HID, 128), BF16),
@@ -453,10 +459,10 @@
 
     for load in loads[:5]:
         load.wait()
-    first_pass(rank, count_ref[0], v, 0)
-    for load in loads[5:]:
-        load.wait()
-    pl.semaphore_wait(barrier, CHIPS + RING - 1)
+    for half in range(2):
+        first_pass(rank, count_ref[0], v, half)
+        if half == 0:
+            v.acc[...] = structure_sum(v, pl.ds(0, YZ), 0)
 
     def share(slots, phase):
         for i in FAR_FIRST:
@@ -465,23 +471,29 @@
     def shared(slots, phase):
         await_bytes(slots.at[pl.ds(0, RING - 1)], sem.ring_r.at[phase])
 
-    share(v.lattice, 0)
-    v.acc[...] = structure_sum(v, 0)
-    first_pass(rank, count_ref[0], v, 1)
-    structure = v.acc[...] + structure_sum(v, 1)
-    v.part[:YZ, :] = structure[:, :128].astype(BF16)
-    v.part[YZ:, :] = structure[:, 128:].astype(BF16)
-
     def half_rows(which):
         return pl.ds(pl.multiple_of(YZ * which, YZ), YZ)
 
     def to_mate(src, dst, phase):
         return remote(src, dst, sem.mate_s.at[phase], sem.mate_r.at[phase], mate)
 
-    swap_parts = to_mate(v.part.at[half_rows(1 - core)], v.mate, 0)
+    def row_sums(which):
+        rows = pl.ds(pl.multiple_of(HALF * which, HALF), HALF)
+        return v.acc[rows, :] + structure_sum(v, rows, 1)
+
+    theirs = row_sums(1 - core)
+    v.part[:HALF, :] = theirs[:, :128].astype(BF16)
+    v.part[HALF:, :] = theirs[:, 128:].astype(BF16)
+    pl.semaphore_wait(barrier, CHIPS + RING - 1)
+    swap_parts = to_mate(v.part, v.mate, 0)
     swap_parts.start()
+    for load in loads[5:]:
+        load.wait()
+    share(v.lattice, 0)
+    mine = row_sums(core)
     swap_parts.wait_recv()
-    v.half[...] = (v.part[half_rows(core)].astype(F32) + v.mate[...].astype(F32)).astype(BF16)
+    v.half[:HALF, :] = (mine[:, :128] + v.mate[:HALF, :].astype(F32)).astype(BF16)
+    v.half[HALF:, :] = (mine[:, 128:] + v.mate[HALF:, :].astype(F32)).astype(BF16)
 
     def pair_rows(which, odd, base=0):
         start = base + PAIR_ROWS * which + (BIG if odd else 0)
@@ -544,11 +556,11 @@
     swap_totals.wait_recv()
 
     coefficients(v)
+    v.charge_ring[ring] = potential_pass(rank, v).astype(BF16)
+    share(v.charge_ring, 2)
     v.up[...] = upstream_table(v)
     v.up_ring[ring] = v.up[pl.ds(pl.multiple_of(64 * core, 64), 64), :]
     share(v.up_ring, 1)
-    v.charge_ring[ring] = potential_pass(rank, v).astype(BF16)
-    share(v.charge_ring, 2)
     molecules = molecule_sums(v)
     for chunk in range(RING):
         v.message[chunk, 3:4, 0:MOLS] = molecules
@@ -661,7 +673,7 @@
     mol, pos, charge, first, middle, last = pl.pallas_call(
         output_kernel,
         out_shape=outs,
-        in_specs=specs(pl.ANY, len(OUTS)),
+        in_specs=specs(pltpu.VMEM, len(OUTS)),
         out_specs=tuple(specs(pl.ANY, len(OUTS))),
         scratch_shapes=[dma((len(OUTS),))],
         compiler_params=pltpu.CompilerParams(vmem_limit_bytes=56 * MIB),

time: 54.4 us -> 44.5 us (0.82)
  Pallas kernels: 52.8 us -> 42.9 us
    pallas_call x1, Pallas kernels: 11.4 us -> 1.79 us  [body(): pl.pallas_call(output_kernel, out_shape=outs, in_specs=specs(pltpu.VMEM,...]
where the time goes in v2:
time: 44.5 us; the launch traced here: 44.3 us
  Pallas kernels  42.9 us (96%)
  between operations  1.45 us (3%)
    pallas_call x1, Pallas kernels, body(): pl.pallas_call(whole_kernel, out_shape=outs, in_specs=specs(pltpu.SMEM, 1...  41.1 us
    pallas_call x1, Pallas kernels, body(): pl.pallas_call(output_kernel, out_shape=outs, in_specs=specs(pltpu.VMEM,...  1.79 us

profile of v2, /device:TPU:1, one launch (start us, length us, event | category | flops | bytes accessed | tf_op | source)
XLA Modules:
  0.0 44.3 jit_solution(8438015903722126614)
XLA Ops:
  1.3 41.1 %ewald.1 = (f32[1,256]{1,0:T(1,128)}, f32[3,512]{1,0:T(4,128)}, f32[32,128]{1,0:T(8,128)}, f32[16,256]{1,0:T(8,128)}, f32[256,256]{1,0:T(8,128)}, /*index=5*/f32[32,256]{1,0:T(8,128)}) custom-call(s32[1]{0:T(128)S(6)} %copy.18.count_ref, f32[3,4096]{1,0:T(4,128)} %pos_ref.1, bf16[4096,128]{1,0:T(8,128)(2,1)} %feat_ref.1, bf16[32,128]{1,0:T(8,128)(2,1)} %bitcast.7, ...), custom_call_target="tpu_custom_call" | custom-call | tf_op jit(solution)/shard_map/ewald/pallas_call | solution.py:658
  42.4 1.8 %outputs.1 = (f32[1,256]{1,0:T(1,128)}, f32[3,512]{1,0:T(4,128)}, f32[32,128]{1,0:T(8,128)}, f32[16,256]{1,0:T(8,128)}, f32[256,256]{1,0:T(8,128)}, /*index=5*/f32[32,256]{1,0:T(8,128)}) custom-call(f32[1,256]{1,0:T(1,128)} %get-tuple-element.18.refs_0_, f32[3,512]{1,0:T(4,128)} %get-tuple-element.19.refs_1_, f32[32,128]{1,0:T(8,128)} %get-tuple-element.20.refs_2_, ...), custom_call_target="tpu_custom_call" | custom-call | tf_op jit(solution)/shard_map/outputs/pallas_call | solution.py:673

commit v3 on v2

--- a/solution.py
+++ b/solution.py
@@ -32,6 +32,10 @@
 SMALL = 32
 TABLE = 512
 FAR_FIRST = (4, 3, 5, 2, 6, 1, 7)
+CHIP_STEPS = sorted(
+    ((dx, dy) for dx in range(4) for dy in range(4) if dx or dy),
+    key=lambda step: -(min(step[0], 4 - step[0]) + min(step[1], 4 - step[1])),
+)
 MIB = 1 << 20
 
 
@@ -143,22 +147,12 @@
     lax.fori_loop(low, high, run, 0)
 
 
-def first_pass(rank, count, v, half):
-    cot_parts = rows_of_parts(v.cot[...])
-    for tile in range(half * TILES // 2, (half + 1) * TILES // 2):
-        at = pl.ds(tile * TILE, TILE)
-        slot = tile * TILE + lax.broadcasted_iota(jnp.int32, (1, TILE), 1)
-        alive = jnp.where(slot < count, 1.0, 0.0)
-        v.alive[:, at] = alive
-        molecule = lax.broadcasted_iota(jnp.int32, (MOLS, TILE), 0)
-        member = jnp.where(molecule == v.ids[:, at], 1.0, 0.0).astype(BF16)
-        v.member[:, at] = member
-        weight = jnp.sum(nn(cot_parts, member), axis=0, keepdims=True)
-        v.weight[:, at] = weight
-        charge = (nt(v.cw[...], v.feat[at, :]) * alive).astype(BF16).astype(F32)
-        pair = jnp.concatenate([charge, weight * charge], axis=0).astype(BF16)
-        v.pair[:, at] = pair
-        pair = pair.astype(F32)
+def half_tiles(half):
+    return [pl.ds(tile * TILE, TILE) for tile in range(half * TILES // 2, (half + 1) * TILES // 2)]
+
+
+def functions(rank, v, half):
+    for at in half_tiles(half):
         turns2, _ = yz_turns(v.pos[1:2, at])
         turns3, _ = yz_turns(v.pos[2:3, at])
         turns1, _ = x_turns(v.pos[0:1, at], rank)
@@ -174,8 +168,36 @@
         v.b[576:624, at] = jnp.concatenate([u3, v.u2[:, at]], axis=0).astype(BF16)
         row = lax.broadcasted_iota(jnp.int32, (16, TILE), 0)
         v.b[624:640, at] = jnp.where(row == 0, 1.0, 0.0).astype(BF16)
+
+
+def charges(count, v, half):
+    cot_parts = rows_of_parts(v.cot[...])
+    for at in half_tiles(half):
+        slot = at.start + lax.broadcasted_iota(jnp.int32, (1, TILE), 1)
+        alive = jnp.where(slot < count, 1.0, 0.0)
+        v.alive[:, at] = alive
+        molecule = lax.broadcasted_iota(jnp.int32, (MOLS, TILE), 0)
+        member = jnp.where(molecule == v.ids[:, at], 1.0, 0.0).astype(BF16)
+        v.member[:, at] = member
+        weight = jnp.sum(nn(cot_parts, member), axis=0, keepdims=True)
+        v.weight[:, at] = weight
+        charge = (nt(v.cw[...], v.feat[at, :]) * alive).astype(BF16).astype(F32)
+        pair = jnp.concatenate([charge, weight * charge], axis=0).astype(BF16)
+        v.pair[:, at] = pair
+        pair = pair.astype(F32)
         for j in range(4):
             v.a[64 * j : 64 * j + 64, at] = (v.u1[j : j + 1, at] * pair).astype(BF16)
+
+
+def derivatives(rank, v):
+    for half in range(2):
+        for at in half_tiles(half):
+            turns1, h1 = x_turns(v.pos[0:1, at], rank)
+            turns2, h2 = yz_turns(v.pos[1:2, at])
+            turns3, h3 = yz_turns(v.pos[2:3, at])
+            v.d1[:, at] = h1 * cos_turns(turns1 + 0.25)
+            v.d2[:, at] = h2 * cos_turns(turns2 + 0.25)
+            v.d3[:, at] = h3 * cos_turns(turns3 + 0.25)
 
 
 def structure_sum(v, rows, half):
@@ -313,30 +335,23 @@
     grad_logits = jnp.where(lane < CH, upstream * v.sigmoid[...], 0.0).astype(BF16)
     out_grad = tn(grad_logits, v.act_two[...])
     grad_two = (nt(grad_logits, v.fout_wide[...]) * v.slope_two[...]).astype(BF16)
-    v.mid_grad[...] = tn(v.act_one[...], grad_two)
+    mid_grad = tn(v.act_one[...], grad_two)
     grad_one = (nt(grad_two, v.fmid[...]) * v.slope_one[...]).astype(BF16)
-    v.in_grad[...] = tn(v.radial[...], grad_one)
-    v.out_grad[...] = out_grad[:CH]
+    return tn(v.radial[...], grad_one), mid_grad, out_grad[:CH]
 
 
 GRAD_SCALE = 0.5 * 2.0 * math.pi / BOX_EDGE
 
 
-def potential_pass(rank, v):
+def potential_pass(v):
     for tile in range(TILES):
         at = pl.ds(tile * TILE, TILE)
-        turns1, h1 = x_turns(v.pos[0:1, at], rank)
-        d1 = h1 * cos_turns(turns1 + 0.25)
         u1 = v.u1[:, at]
-        pair = v.pair[:, at].astype(F32)
-        charge, weighted = pair[:CH], pair[CH:]
         w = nn(v.gt[...], v.b[:, at])
+        v.w[:, at] = w
         pot = sum(u1[j : j + 1, :] * w[64 * j : 64 * j + 64, :] for j in range(4))
-        potx = sum(d1[j : j + 1, :] * w[64 * j : 64 * j + 64, :] for j in range(4))
         volt, other = pot[:CH], pot[CH:]
-        grad_x = jnp.sum(weighted * potx[:CH] + charge * potx[CH:], axis=0, keepdims=True)
-        v.message[tile, 0:1, :] = grad_x * GRAD_SCALE
-        v.energy[:, at] = 0.5 * jnp.sum(charge * volt, axis=0, keepdims=True)
+        v.volt[:, at] = volt
         v.cot_rows[:, at] = (0.5 * (v.weight[:, at] * volt + other) * v.alive[:, at]).astype(BF16)
     return nn(v.cot_rows[...], v.feat[...])
 
@@ -351,17 +366,20 @@
 
     for tile in range(TILES):
         at = pl.ds(tile * TILE, TILE)
-        turns2, h2 = yz_turns(v.pos[1:2, at])
-        turns3, h3 = yz_turns(v.pos[2:3, at])
-        v.d2[:, at] = h2 * cos_turns(turns2 + 0.25)
         v.response[:, at] = nn(v.gs[...], v.a[:, at])
-        u3, d3 = v.u3[:, at], h3 * cos_turns(turns3 + 0.25)
+        pair = v.pair[:, at].astype(F32)
+        charge, weighted = pair[:CH], pair[CH:]
+        v.energy[:, at] = 0.5 * jnp.sum(charge * v.volt[:, at], axis=0, keepdims=True)
+        potx = sum(v.d1[j : j + 1, at] * v.w[64 * j : 64 * j + 64, at] for j in range(4))
+        grad_x = jnp.sum(weighted * potx[:CH] + charge * potx[CH:], axis=0, keepdims=True)
+        u3, d3 = v.u3[:, at], v.d3[:, at]
         sum_y = fold(v.d2[:, at] * v.response[600:624, at])
         sum_z = fold(d3 * v.response[576:600, at])
         for y in range(24):
             response = v.response[24 * y : 24 * y + 24, at]
             sum_y = sum_y + v.d2[y : y + 1, at] * fold(u3 * response)
             sum_z = sum_z + v.u2[y : y + 1, at] * fold(d3 * response)
+        v.message[tile, 0:1, :] = grad_x * GRAD_SCALE
         v.message[tile, 1:2, :] = jnp.sum(sum_y, axis=0, keepdims=True) * GRAD_SCALE
         v.message[tile, 2:3, :] = jnp.sum(sum_z, axis=0, keepdims=True) * GRAD_SCALE
 
@@ -370,7 +388,8 @@
     pos=((3, CAP), F32), feat=((CAP, 128), BF16), cw=((CH, 128), BF16), ids=((1, CAP), jnp.int32),
     cot=((1, MOLS), F32), fin=((16, HID), BF16), fmid=((HID, HID), BF16), fout=((CH, HID), BF16),
     signs=((2 * HALF, YZ), BF16), signs_t=((YZ, 2 * HALF), BF16), lattice=((RING, 3, 1024), jnp.int32),
-    u1=((8, CAP), F32), u2=((24, CAP), F32), u3=((24, CAP), F32), d2=((24, CAP), F32),
+    u1=((8, CAP), F32), u2=((24, CAP), F32), u3=((24, CAP), F32), d1=((8, CAP), F32), d2=((24, CAP), F32), d3=((24, CAP), F32),
+    w=((XC, CAP), F32), volt=((CH, CAP), F32),
     alive=((1, CAP), F32), weight=((1, CAP), F32), member=((MOLS, CAP), BF16),
     pair=((2 * CH, CAP), BF16), b=((YZ, CAP), BF16), a=((XC, CAP), BF16), acc=((YZ, XC), F32),
     part=((YZ, 128), BF16), mate=((YZ, 128), BF16), half=((YZ, 128), BF16),
@@ -385,11 +404,9 @@
     message=((RING, 4, TILE), F32), message_box=((RING, 4, TILE), F32),
     charge_ring=((RING, CH, 128), BF16), charge_mine=((CH, 128), BF16), charge_mate=((CH, 128), BF16),
     charge_plane=((CHIPS, CH, 128), BF16),
-    mol_sum=((1, MOLS), F32), pos_sum=((3, TILE), F32), charge_sum=((CH, 128), F32),
-    in_grad=((16, HID), F32), mid_grad=((HID, HID), F32), out_grad=((CH, HID), F32),
 )
 SEMAPHORES = dict(
-    load=11, store=6, mate_s=4, mate_r=4, scatter_s=1, scatter_r=1, gather_s=1, gather_r=1,
+    load=11, mate_s=4, mate_r=4, scatter_s=1, scatter_r=1, gather_s=1, gather_r=1,
     ring_s=4, ring_r=4, plane_s=1, plane_r=1,
 )
 OUTS = (
@@ -423,14 +440,6 @@
     ]
     for load in loads:
         load.start()
-    stores = [
-        pltpu.make_async_copy(src, dst, sem.store.at[i])
-        for i, (src, dst) in enumerate((
-            (v.mol_sum, mol_out), (v.pos_sum, pos_out), (v.charge_sum, charge_out),
-            (v.in_grad, in_out), (v.mid_grad, mid_out), (v.out_grad, out_out),
-        ))
-    ]
-
     def remote(src, dst, send, recv, device):
         return pltpu.make_async_remote_copy(
             src_ref=src, dst_ref=dst, send_sem=send, recv_sem=recv,
@@ -446,6 +455,9 @@
     def chip_device(which):
         return (2 * which + core, ring)
 
+    def chip_at(step):
+        return 4 * lax.rem(chip // 4 + step[0], 4) + lax.rem(lax.rem(chip, 4) + step[1], 4)
+
     mate = (plane + 1 - 2 * core, ring)
 
     barrier = pltpu.get_barrier_semaphore()
@@ -457,12 +469,14 @@
     loop(1, RING, lambda i: greet(ring_peer(i)))
     greet(mate)
 
-    for load in loads[:5]:
+    loads[0].wait()
+    functions(rank, v, 0)
+    for load in loads[1:5]:
         load.wait()
-    for half in range(2):
-        first_pass(rank, count_ref[0], v, half)
-        if half == 0:
-            v.acc[...] = structure_sum(v, pl.ds(0, YZ), 0)
+    charges(count_ref[0], v, 0)
+    v.acc[...] = structure_sum(v, pl.ds(0, YZ), 0)
+    functions(rank, v, 1)
+    charges(count_ref[0], v, 1)
 
     def share(slots, phase):
         for i in FAR_FIRST:
@@ -499,23 +513,21 @@
         start = base + PAIR_ROWS * which + (BIG if odd else 0)
         return pl.ds(pl.multiple_of(start, 16), SMALL if odd else BIG)
 
-    def scatter(pair, odd):
-        size = SMALL if odd else BIG
-        remote(
-            v.half.at[pair_rows(pair, odd)], v.inbox.at[chip, pl.ds(0, size)],
-            sem.scatter_s.at[0], sem.scatter_r.at[0], chip_device(2 * pair + odd),
-        ).start()
-
     my_pair, my_odd = chip // 2, lax.rem(chip, 2)
 
-    def scatter_pair(i):
-        pair = lax.rem(my_pair + 1 + lax.rem(i + 3, 7), 8)
-        scatter(pair, 0)
-        scatter(pair, 1)
-
-    loop(0, 7, scatter_pair)
-    pl.when(my_odd == 0)(lambda: scatter(my_pair, 1))
-    pl.when(my_odd == 1)(lambda: scatter(my_pair, 0))
+    def scatter(odd):
+        for step in CHIP_STEPS:
+            other = chip_at(step)
+            other_odd = (odd + step[1]) % 2
+            size = SMALL if other_odd else BIG
+            remote(
+                v.half.at[pair_rows(other // 2, other_odd)], v.inbox.at[chip, pl.ds(0, size)],
+                sem.scatter_s.at[0], sem.scatter_r.at[0], chip_device(other),
+            ).start()
+
+    pl.when(my_odd == 0)(lambda: scatter(0))
+    pl.when(my_odd == 1)(lambda: scatter(1))
+    derivatives(rank, v)
     filter_forward(rank, v)
     table_forward(rank, v)
 
@@ -529,14 +541,11 @@
         rows = pair_rows(my_pair, odd, YZ * core)
         v.total[rows] = value.astype(BF16)
 
-        def send(i):
-            other = lax.rem(chip + 1 + lax.rem(i + 5, 15), CHIPS)
+        for step in CHIP_STEPS:
             remote(
                 v.total.at[rows], v.total.at[rows], sem.gather_s.at[0], sem.gather_r.at[0],
-                chip_device(other),
+                chip_device(chip_at(step)),
             ).start()
-
-        loop(0, CHIPS - 1, send)
 
     pl.when(my_odd == 0)(lambda: reduce(0))
     pl.when(my_odd == 1)(lambda: reduce(1))
@@ -556,18 +565,19 @@
     swap_totals.wait_recv()
 
     coefficients(v)
-    v.charge_ring[ring] = potential_pass(rank, v).astype(BF16)
+    v.charge_ring[ring] = potential_pass(v).astype(BF16)
     share(v.charge_ring, 2)
     v.up[...] = upstream_table(v)
-    v.up_ring[ring] = v.up[pl.ds(pl.multiple_of(64 * core, 64), 64), :]
+    up_rows = pl.ds(pl.multiple_of(64 * core, 64), 64)
+    v.up_ring[ring] = v.up[up_rows, :]
     share(v.up_ring, 1)
+
+    swapped_coefficients(v)
+    force_pass(v)
     molecules = molecule_sums(v)
     for chunk in range(RING):
         v.message[chunk, 3:4, 0:MOLS] = molecules
         v.message[chunk, 3:4, MOLS:TILE] = jnp.zeros((1, TILE - MOLS), F32)
-
-    swapped_coefficients(v)
-    force_pass(v)
     for i in FAR_FIRST:
         peer = lax.rem(ring + i, RING)
         remote(v.message.at[peer], v.message_box.at[ring], sem.ring_s.at[3], sem.ring_r.at[3], ring_peer(i)).start()
@@ -578,12 +588,6 @@
         for slot in range(1, slots.shape[0]):
             value = value + slots[slot].astype(F32)
         return value
-
-    shared(v.up_ring, 1)
-    up_rows = pl.ds(pl.multiple_of(64 * core, 64), 64)
-    v.up_total[up_rows, :] = added(v.up_ring).astype(BF16)
-    swap_up = to_mate(v.up_total.at[up_rows], v.up_total.at[up_rows], 2)
-    swap_up.start()
 
     shared(v.charge_ring, 2)
     v.charge_mine[...] = added(v.charge_ring).astype(BF16)
@@ -591,26 +595,22 @@
     swap_charge.start()
     swap_charge.wait_recv()
     v.charge_plane[chip] = (v.charge_mine[...].astype(F32) + v.charge_mate[...].astype(F32)).astype(BF16)
-
-    def charge_to_plane(i):
-        other = lax.rem(chip + 1 + lax.rem(i + 5, 15), CHIPS)
+    for step in CHIP_STEPS:
         remote(
             v.charge_plane.at[chip], v.charge_plane.at[chip], sem.plane_s.at[0], sem.plane_r.at[0],
-            chip_device(other),
+            chip_device(chip_at(step)),
         ).start()
 
-    loop(0, CHIPS - 1, charge_to_plane)
-
+    shared(v.up_ring, 1)
+    v.up_total[up_rows, :] = added(v.up_ring).astype(BF16)
+    swap_up = to_mate(v.up_total.at[up_rows], v.up_total.at[up_rows], 2)
+    swap_up.start()
     swap_up.wait_recv()
-    filter_backward(v)
-    for store in stores[3:]:
-        store.start()
+    in_out[...], mid_out[...], out_out[...] = filter_backward(v)
     shared(v.message_box, 3)
     value = added(v.message_box)
-    v.pos_sum[...] = value[0:3]
-    v.mol_sum[...] = value[3:4, :MOLS]
-    for store in stores[:2]:
-        store.start()
+    pos_out[...] = value[0:3]
+    mol_out[...] = value[3:4, :MOLS]
 
     for swap in (swap_parts, swap_totals, swap_up, swap_charge):
         swap.wait_send()
@@ -626,10 +626,7 @@
     await_bytes(v.charge_plane.at[pl.ds(0, CHIPS - 1)], sem.plane_s.at[0])
 
     await_bytes(v.charge_plane.at[pl.ds(0, CHIPS - 1)], sem.plane_r.at[0])
-    v.charge_sum[...] = added(v.charge_plane)
-    stores[2].start()
-    for store in stores:
-        store.wait()
+    charge_out[...] = added(v.charge_plane)
 
 
 def output_kernel(*refs):
@@ -657,9 +654,9 @@
     outs = tuple(shape(*out) for out in OUTS)
     sums = pl.pallas_call(
         whole_kernel,
-        out_shape=outs,
+        out_shape=tuple(pltpu.VMEM(*out) for out in OUTS),
         in_specs=specs(pltpu.SMEM, 1) + specs(pl.ANY, 11),
-        out_specs=tuple(specs(pl.ANY, len(OUTS))),
+        out_specs=tuple(specs(pltpu.VMEM, len(OUTS))),
         scratch_shapes=[pltpu.VMEM(dims, kind) for dims, kind in SCRATCH.values()]
         + [dma((count,)) for count in SEMAPHORES.values()],
         compiler_params=pltpu.CompilerParams(
@@ -678,7 +675,7 @@
         scratch_shapes=[dma((len(OUTS),))],
         compiler_params=pltpu.CompilerParams(vmem_limit_bytes=56 * MIB),
         name="outputs",
-    )(*sums)
+    )(*[pltpu.with_memory_space_constraint(value, pltpu.VMEM) for value in sums])
     return (mol.reshape(MOLS), pos, charge.T, first, middle, last.T)
 
 

time: 44.5 us -> 39.3 us (0.88)
  Pallas kernels: 42.9 us -> 37.7 us
    pallas_call x1, Pallas kernels: 41.1 us -> 37 us  [body(): pl.pallas_call(whole_kernel, out_shape=tuple((pltpu.VMEM(*out) for out in...]
    pallas_call x1, Pallas kernels: 1.79 us -> 0.78 us  [body(): pl.pallas_call(output_kernel, out_shape=outs, in_specs=specs(pltpu.VMEM,...]
where the time goes in v3:
time: 39.3 us; the launch traced here: 39.2 us
  Pallas kernels  37.7 us (96%)
  between operations  1.45 us (4%)
    pallas_call x1, Pallas kernels, body(): pl.pallas_call(whole_kernel, out_shape=tuple((pltpu.VMEM(*out) for out in...  37 us

profile of v3, /device:TPU:1, one launch (start us, length us, event | category | flops | bytes accessed | tf_op | source)
XLA Modules:
  0.0 39.2 jit_solution(7892997522020649927)
XLA Ops:
  1.3 37.0 %ewald.1 = (f32[1,256]{1,0:T(1,128)S(1)}, f32[3,512]{1,0:T(4,128)S(1)}, f32[32,128]{1,0:T(8,128)S(1)}, f32[16,256]{1,0:T(8,128)S(1)}, f32[256,256]{1,0:T(8,128)S(1)}, /*index=5*/f32[32,256]{1,0:T(8,128)S(1)}) custom-call(s32[1]{0:T(128)S(6)} %copy.18.count_ref, f32[3,4096]{1,0:T(4,128)} %pos_ref.1, bf16[4096,128]{1,0:T(8,128)(2,1)} %feat_ref.1, ...), custom_call_target="tpu_custom_call" | custom-call | tf_op jit(solution)/shard_map/ewald/pallas_call | solution.py:655
  38.2 0.8 %outputs.1 = (f32[1,256]{1,0:T(1,128)}, f32[3,512]{1,0:T(4,128)}, f32[32,128]{1,0:T(8,128)}, f32[16,256]{1,0:T(8,128)}, f32[256,256]{1,0:T(8,128)}, /*index=5*/f32[32,256]{1,0:T(8,128)}) custom-call(f32[1,256]{1,0:T(1,128)S(1)} %get-tuple-element.18.refs_0_, f32[3,512]{1,0:T(4,128)S(1)} %get-tuple-element.19.refs_1_, ...), custom_call_target="tpu_custom_call" | custom-call | tf_op jit(solution)/shard_map/outputs/pallas_call | solution.py:670

commit v4 on v3

--- a/solution.py
+++ b/solution.py
@@ -192,6 +192,7 @@
 def derivatives(rank, v):
     for half in range(2):
         for at in half_tiles(half):
+            v.member_t[at, :] = v.member[:, at].T
             turns1, h1 = x_turns(v.pos[0:1, at], rank)
             turns2, h2 = yz_turns(v.pos[1:2, at])
             turns3, h3 = yz_turns(v.pos[2:3, at])
@@ -273,6 +274,8 @@
     lane = lax.broadcasted_iota(jnp.int32, (HALF, 128), 1)
     v.both[...] = jnp.where(lane < 64, counted[:, 0:1], counted[:, 1:2])
     v.difference[...] = jnp.where(lane < 64, counted[:, 2:3], counted[:, 3:4])
+    v.filter_both[...] = v.filters[...] * v.both[...]
+    v.filter_difference[...] = v.filters[...] * v.difference[...]
 
 
 def coefficients(v):
@@ -287,8 +290,7 @@
     v.sums[...] = nn(signs, total)
     ncc, ncs = v.sums[:HALF, :128], v.sums[HALF:, :128]
     nsc, nss = v.sums[:HALF, 128:], v.sums[HALF:, 128:]
-    filters = v.filters[...]
-    fp, fd = filters * v.both[...], filters * v.difference[...]
+    fp, fd = v.filter_both[...], v.filter_difference[...]
     gcc = (fp * ncc - fd * nss).astype(BF16)
     gss = (fp * nss - fd * ncc).astype(BF16)
     gsc = (fp * nsc + fd * ncs).astype(BF16)
@@ -357,7 +359,7 @@
 
 
 def molecule_sums(v):
-    return jnp.sum(nt(rows_of_parts(v.energy[...]), v.member[...]), axis=0, keepdims=True)
+    return jnp.sum(nn(rows_of_parts(v.energy[...]), v.member_t[...]), axis=0, keepdims=True)
 
 
 def force_pass(v):
@@ -390,7 +392,7 @@
     signs=((2 * HALF, YZ), BF16), signs_t=((YZ, 2 * HALF), BF16), lattice=((RING, 3, 1024), jnp.int32),
     u1=((8, CAP), F32), u2=((24, CAP), F32), u3=((24, CAP), F32), d1=((8, CAP), F32), d2=((24, CAP), F32), d3=((24, CAP), F32),
     w=((XC, CAP), F32), volt=((CH, CAP), F32),
-    alive=((1, CAP), F32), weight=((1, CAP), F32), member=((MOLS, CAP), BF16),
+    alive=((1, CAP), F32), weight=((1, CAP), F32), member=((MOLS, CAP), BF16), member_t=((CAP, MOLS), BF16),
     pair=((2 * CH, CAP), BF16), b=((YZ, CAP), BF16), a=((XC, CAP), BF16), acc=((YZ, XC), F32),
     part=((YZ, 128), BF16), mate=((YZ, 128), BF16), half=((YZ, 128), BF16),
     inbox=((CHIPS, BIG, 128), BF16), total=((2 * YZ, 128), BF16),
@@ -398,6 +400,7 @@
     slope_one=((TABLE, HID), F32), slope_two=((TABLE, HID), F32), fout_wide=((HID, 128), BF16),
     sigmoid=((TABLE, 128), F32), same=((TABLE, 2 * HALF), BF16), filters=((HALF, 128), F32),
     both=((HALF, 128), F32), difference=((HALF, 128), F32),
+    filter_both=((HALF, 128), F32), filter_difference=((HALF, 128), F32),
     sums=((2 * HALF, XC), F32), coef=((2 * HALF, XC), BF16), energy=((1, CAP), F32), cot_rows=((CH, CAP), BF16),
     gt=((XC, YZ), BF16), gs=((YZ, XC), BF16), response=((YZ, CAP), F32),
     up=((128, 128), BF16), up_ring=((RING, 64, 128), BF16), up_total=((128, 128), BF16),
@@ -574,6 +577,16 @@
 
     swapped_coefficients(v)
     force_pass(v)
+    def added(slots):
+        value = slots[0].astype(F32)
+        for slot in range(1, slots.shape[0]):
+            value = value + slots[slot].astype(F32)
+        return value
+
+    shared(v.charge_ring, 2)
+    v.charge_mine[...] = added(v.charge_ring).astype(BF16)
+    swap_charge = to_mate(v.charge_mine, v.charge_mate, 3)
+    swap_charge.start()
     molecules = molecule_sums(v)
     for chunk in range(RING):
         v.message[chunk, 3:4, 0:MOLS] = molecules
@@ -582,17 +595,6 @@
         peer = lax.rem(ring + i, RING)
         remote(v.message.at[peer], v.message_box.at[ring], sem.ring_s.at[3], sem.ring_r.at[3], ring_peer(i)).start()
     v.message_box[ring] = v.message[ring]
-
-    def added(slots):
-        value = slots[0].astype(F32)
-        for slot in range(1, slots.shape[0]):
-            value = value + slots[slot].astype(F32)
-        return value
-
-    shared(v.charge_ring, 2)
-    v.charge_mine[...] = added(v.charge_ring).astype(BF16)
-    swap_charge = to_mate(v.charge_mine, v.charge_mate, 3)
-    swap_charge.start()
     swap_charge.wait_recv()
     v.charge_plane[chip] = (v.charge_mine[...].astype(F32) + v.charge_mate[...].astype(F32)).astype(BF16)
     for step in CHIP_STEPS:

time: 39.3 us -> 40.3 us (1.025)
  Pallas kernels: 37.7 us -> 38.8 us
    pallas_call x1, Pallas kernels: 37 us -> 38 us  [body(): pl.pallas_call(whole_kernel, out_shape=tuple((pltpu.VMEM(*out) for out in...]
where the time goes in v4:
time: 40.3 us; the launch traced here: 40.2 us
  Pallas kernels  38.8 us (96%)
  between operations  1.45 us (4%)
    pallas_call x1, Pallas kernels, body(): pl.pallas_call(whole_kernel, out_shape=tuple((pltpu.VMEM(*out) for out in...  38 us

profile of v4, /device:TPU:1, one launch (start us, length us, event | category | flops | bytes accessed | tf_op | source)
XLA Modules:
  0.0 40.2 jit_solution(3163380540948988032)
XLA Ops:
  1.3 38.0 %ewald.1 = (f32[1,256]{1,0:T(1,128)S(1)}, f32[3,512]{1,0:T(4,128)S(1)}, f32[32,128]{1,0:T(8,128)S(1)}, f32[16,256]{1,0:T(8,128)S(1)}, f32[256,256]{1,0:T(8,128)S(1)}, /*index=5*/f32[32,256]{1,0:T(8,128)S(1)}) custom-call(s32[1]{0:T(128)S(6)} %copy.18.count_ref, f32[3,4096]{1,0:T(4,128)} %pos_ref.1, bf16[4096,128]{1,0:T(8,128)(2,1)} %feat_ref.1, ...), custom_call_target="tpu_custom_call" | custom-call | tf_op jit(solution)/shard_map/ewald/pallas_call | solution.py:657
  39.3 0.8 %outputs.1 = (f32[1,256]{1,0:T(1,128)}, f32[3,512]{1,0:T(4,128)}, f32[32,128]{1,0:T(8,128)}, f32[16,256]{1,0:T(8,128)}, f32[256,256]{1,0:T(8,128)}, /*index=5*/f32[32,256]{1,0:T(8,128)}) custom-call(f32[1,256]{1,0:T(1,128)S(1)} %get-tuple-element.18.refs_0_, f32[3,512]{1,0:T(4,128)S(1)} %get-tuple-element.19.refs_1_, ...), custom_call_target="tpu_custom_call" | custom-call | tf_op jit(solution)/shard_map/outputs/pallas_call | solution.py:672

commit v5 on v3

--- a/solution.py
+++ b/solution.py
@@ -273,6 +273,8 @@
     lane = lax.broadcasted_iota(jnp.int32, (HALF, 128), 1)
     v.both[...] = jnp.where(lane < 64, counted[:, 0:1], counted[:, 1:2])
     v.difference[...] = jnp.where(lane < 64, counted[:, 2:3], counted[:, 3:4])
+    v.filter_both[...] = v.filters[...] * v.both[...]
+    v.filter_difference[...] = v.filters[...] * v.difference[...]
 
 
 def coefficients(v):
@@ -287,8 +289,7 @@
     v.sums[...] = nn(signs, total)
     ncc, ncs = v.sums[:HALF, :128], v.sums[HALF:, :128]
     nsc, nss = v.sums[:HALF, 128:], v.sums[HALF:, 128:]
-    filters = v.filters[...]
-    fp, fd = filters * v.both[...], filters * v.difference[...]
+    fp, fd = v.filter_both[...], v.filter_difference[...]
     gcc = (fp * ncc - fd * nss).astype(BF16)
     gss = (fp * nss - fd * ncc).astype(BF16)
     gsc = (fp * nsc + fd * ncs).astype(BF16)
@@ -398,6 +399,7 @@
     slope_one=((TABLE, HID), F32), slope_two=((TABLE, HID), F32), fout_wide=((HID, 128), BF16),
     sigmoid=((TABLE, 128), F32), same=((TABLE, 2 * HALF), BF16), filters=((HALF, 128), F32),
     both=((HALF, 128), F32), difference=((HALF, 128), F32),
+    filter_both=((HALF, 128), F32), filter_difference=((HALF, 128), F32),
     sums=((2 * HALF, XC), F32), coef=((2 * HALF, XC), BF16), energy=((1, CAP), F32), cot_rows=((CH, CAP), BF16),
     gt=((XC, YZ), BF16), gs=((YZ, XC), BF16), response=((YZ, CAP), F32),
     up=((128, 128), BF16), up_ring=((RING, 64, 128), BF16), up_total=((128, 128), BF16),

time: 39.3 us -> 39.3 us (level)
  no operation moved by 1% of the time
where the time goes in v5:
time: 39.3 us; the launch traced here: 39.2 us
  Pallas kernels  37.7 us (96%)
  between operations  1.45 us (4%)
    pallas_call x1, Pallas kernels, body(): pl.pallas_call(whole_kernel, out_shape=tuple((pltpu.VMEM(*out) for out in...  36.9 us

profile of v5, /device:TPU:1, one launch (start us, length us, event | category | flops | bytes accessed | tf_op | source)
XLA Modules:
  0.0 39.2 jit_solution(2436200639010484408)
XLA Ops:
  1.3 36.9 %ewald.1 = (f32[1,256]{1,0:T(1,128)S(1)}, f32[3,512]{1,0:T(4,128)S(1)}, f32[32,128]{1,0:T(8,128)S(1)}, f32[16,256]{1,0:T(8,128)S(1)}, f32[256,256]{1,0:T(8,128)S(1)}, /*index=5*/f32[32,256]{1,0:T(8,128)S(1)}) custom-call(s32[1]{0:T(128)S(6)} %copy.18.count_ref, f32[3,4096]{1,0:T(4,128)} %pos_ref.1, bf16[4096,128]{1,0:T(8,128)(2,1)} %feat_ref.1, ...), custom_call_target="tpu_custom_call" | custom-call | tf_op jit(solution)/shard_map/ewald/pallas_call | solution.py:657
  38.2 0.8 %outputs.1 = (f32[1,256]{1,0:T(1,128)}, f32[3,512]{1,0:T(4,128)}, f32[32,128]{1,0:T(8,128)}, f32[16,256]{1,0:T(8,128)}, f32[256,256]{1,0:T(8,128)}, /*index=5*/f32[32,256]{1,0:T(8,128)}) custom-call(f32[1,256]{1,0:T(1,128)S(1)} %get-tuple-element.18.refs_0_, f32[3,512]{1,0:T(4,128)S(1)} %get-tuple-element.19.refs_1_, ...), custom_call_target="tpu_custom_call" | custom-call | tf_op jit(solution)/shard_map/outputs/pallas_call | solution.py:672
